TPU v7x, 256 devices: a whole 4x4x8 slice. The times are simulated.
256 devices in a mesh: ctx: 64 (over z, y, core), dp: 4 (over x).
Axes of the slice: x: 4, y: 4, z: 8, core: 2. Of those that a mesh axis runs over, the one named last changes fastest.
Arguments:
- queries: bfloat16 [32768, 2048], P(('dp', 'ctx')), parts along dimension 0, may hold values from -6 to 6
- keys: bfloat16 [32768, 512], P(('dp', 'ctx')), parts along dimension 0, may hold values from -6 to 6
- values: bfloat16 [32768, 512], P(('dp', 'ctx')), parts along dimension 0, may hold values from -6 to 6
- outputs: bfloat16 [32768, 2048], P(('dp', 'ctx')), parts along dimension 0, may hold values from -6 to 6
- out_grad: bfloat16 [32768, 2048], P(('dp', 'ctx')), parts along dimension 0, may hold values from -6 to 6
- log_sum_exp: float32 [16, 32768], P(None, ('dp', 'ctx')), parts along dimension 1
- spans: int32 [16], P('dp'), parts along dimension 0, may hold values from 257 to 8192, as said below
Outputs:
- grad_queries: bfloat16 [32768, 2048], P(('dp', 'ctx')), parts along dimension 0
- grad_keys: bfloat16 [32768, 512], P(('dp', 'ctx')), parts along dimension 0
- grad_values: bfloat16 [32768, 512], P(('dp', 'ctx')), parts along dimension 0
There are 4 independent parts, one for each index of `dp`. A program takes and returns all parts, laid end to end along the dimension named above; each array names one. Nothing has to cross between parts.
Inputs may be any that keep to these rules, and one draw needn't show every extreme that they name: `spans`: in some order, one key-value head has a span above 256 and at most 512, one above 1024 and at most 2048, one above 2048 and at most 4096, and one exactly 8192.
All inputs are finite; a program needn't handle non-finite values.
Results may differ from a plain program's by a relative error of at most 0.0058.
Values may be sent and summed in bfloat16 or wider, within the bound.
A program may use at most 64 MiB of HBM per device.

v0:
```python
import math

import jax
import jax.numpy as jnp
from jax import lax
from jax.sharding import PartitionSpec as P

Q_HEADS = 16
KV_HEADS = 4
HEAD_DIM = 128


def shifted(value, axis, steps):
    count = lax.axis_size(axis)
    initial, last = (max(0, -steps), min(count, count - steps))
    return lax.ppermute(value, axis, [(source, source + steps) for source in range(initial, last)])


def shifted_2(x, axis, by):
    count = lax.axis_size(axis)
    return lax.ppermute(x, axis, [(i, (i + by) % count) for i in range(count)])


def score_grads(context, key_rows, value_rows, key_first):
    query_rows, grad_rows, lse_rows, delta_rows, own_first, span_value = context
    scaling = 1.0 / math.sqrt(query_rows.shape[2])
    scores = (
        jnp.einsum("tgd,sd->gts", query_rows, key_rows, preferred_element_type=jnp.float32)
        * scaling
    )
    row_index = own_first + jnp.arange(query_rows.shape[0], dtype=jnp.int32)
    col_index = key_first + jnp.arange(key_rows.shape[0], dtype=jnp.int32)
    distance = row_index[:, None] - col_index[None, :]
    allowed = (distance >= 0) & (distance < span_value)
    probability = jnp.exp(jnp.where(allowed[None], scores - lse_rows[:, :, None], -1e30))
    rounded = probability.astype(jnp.bfloat16)
    dprobs = jnp.einsum("tgd,sd->gts", grad_rows, value_rows, preferred_element_type=jnp.float32)
    dscores = (probability * (dprobs - delta_rows[:, :, None]) * scaling).astype(jnp.bfloat16)
    return (dscores, rounded)


def query_part(key_rows, dscores):
    return jnp.einsum("gts,sd->tgd", dscores, key_rows, preferred_element_type=jnp.float32)


def key_part(context, dscores, rounded):
    key_grad = jnp.einsum("gts,tgd->sd", dscores, context[0], preferred_element_type=jnp.float32)
    value_grad = jnp.einsum("gts,tgd->sd", rounded, context[1], preferred_element_type=jnp.float32)
    return jnp.stack([key_grad, value_grad])


def head_pass(context, key_rows, value_rows, key_first):
    dscores, rounded = score_grads(context, key_rows, value_rows, key_first)
    return (query_part(key_rows, dscores), key_part(context, dscores, rounded))


def chain_window(context, key_rows, value_rows, reach, tok_count, position):
    own_first = context[4]
    local_query, local_keys = head_pass(context, key_rows, value_rows, own_first)
    moving = jnp.stack([key_rows, value_rows])

    def advance(turn_index, carry):
        moving_now, totals, query_total = carry
        moving_now = shifted(moving_now, "ctx", 1)
        totals = shifted_2(totals, "ctx", 1)
        source = position - turn_index - 1

        def compute(operand):
            return head_pass(context, operand[0], operand[1], source * tok_count)

        def nothing(operand):
            return (jnp.zeros_like(local_query), jnp.zeros_like(local_keys))

        query_piece, key_piece = lax.cond(source >= 0, compute, nothing, moving_now)
        return (moving_now, totals + key_piece, query_total + query_piece)

    final = lax.fori_loop(0, reach, advance, (moving, local_keys, local_query))
    home = shifted_2(final[1].astype(jnp.bfloat16), "ctx", -reach).astype(jnp.float32)
    return (final[2], home)


def per_device(queries, keys, values, outputs, out_grad, log_sum_exp, spans):
    tok_count = queries.shape[0]
    devices = lax.axis_size("ctx")
    position = lax.axis_index("ctx")
    head_dim = HEAD_DIM
    group = Q_HEADS // KV_HEADS
    sequence = tok_count * devices
    delta_all = jnp.sum(
        (out_grad.astype(jnp.float32) * outputs.astype(jnp.float32)).reshape(
            tok_count, Q_HEADS, head_dim
        ),
        axis=2,
    ).T
    top_list = [sequence // 16, sequence // 4, sequence // 2, sequence]
    grad_queries = jnp.zeros_like(queries)
    grad_keys = jnp.zeros_like(keys)
    grad_values = jnp.zeros_like(values)
    head_numbers = jnp.arange(KV_HEADS, dtype=jnp.int32)
    prepared = []
    for class_index in range(len(top_list)):
        top_span = top_list[class_index]
        reach = min(devices - 1, -(-top_span // tok_count))
        if class_index == 3:
            inside = spans == sequence
        else:
            inside = (spans > top_span // 2) & (spans <= top_span)
        key_head = jnp.sum(jnp.where(inside, head_numbers, 0))
        span_value = jnp.sum(jnp.where(inside, spans, 0))
        query_cols = key_head * (group * head_dim)
        query_rows = lax.dynamic_slice_in_dim(queries, query_cols, group * head_dim, 1).reshape(
            tok_count, group, head_dim
        )
        grad_rows = lax.dynamic_slice_in_dim(out_grad, query_cols, group * head_dim, 1).reshape(
            tok_count, group, head_dim
        )
        lse_rows = lax.dynamic_slice_in_dim(log_sum_exp, key_head * group, group, 0)
        delta_rows = lax.dynamic_slice_in_dim(delta_all, key_head * group, group, 0)
        key_rows = lax.dynamic_slice_in_dim(keys, key_head * head_dim, head_dim, 1)
        value_rows = lax.dynamic_slice_in_dim(values, key_head * head_dim, head_dim, 1)
        context = (query_rows, grad_rows, lse_rows, delta_rows, position * tok_count, span_value)
        prepared.append((context, key_rows, value_rows, reach, key_head, class_index == 3))
    outcome = []
    cycle_heads = []
    for head in prepared:
        cycle_heads.append(head)
        outcome.append(None)
    cycle_results = [
        chain_window(head[0], head[1], head[2], head[3], tok_count, position)
        for head in cycle_heads
    ]
    placed = 0
    for index in range(len(prepared)):
        outcome[index] = cycle_results[placed]
        placed = placed + 1
    for index in range(len(prepared)):
        key_head = prepared[index][4]
        query_grad, key_grad = outcome[index]
        query_cols = key_head * (group * head_dim)
        grad_queries = lax.dynamic_update_slice_in_dim(
            grad_queries,
            query_grad.reshape(tok_count, group * head_dim).astype(jnp.bfloat16),
            query_cols,
            1,
        )
        grad_keys = lax.dynamic_update_slice_in_dim(
            grad_keys, key_grad[0].astype(jnp.bfloat16), key_head * head_dim, 1
        )
        grad_values = lax.dynamic_update_slice_in_dim(
            grad_values, key_grad[1].astype(jnp.bfloat16), key_head * head_dim, 1
        )
    return (grad_queries, grad_keys, grad_values)


def solution(mesh):
    in_specs = (
        P(("dp", "ctx"), None),
        P(("dp", "ctx"), None),
        P(("dp", "ctx"), None),
        P(("dp", "ctx"), None),
        P(("dp", "ctx"), None),
        P(None, ("dp", "ctx")),
        P("dp"),
    )
    out_specs = (P(("dp", "ctx"), None), P(("dp", "ctx"), None), P(("dp", "ctx"), None))
    return jax.shard_map(
        per_device, mesh=mesh, in_specs=in_specs, out_specs=out_specs, check_vma=False
    )
```

profile of v0, /device:TPU:103, one launch (start us, length us, event | category | flops | bytes accessed | tf_op | source)
XLA Modules:
  0.0 1215.9 jit_solution(439997317526283020)
XLA Ops:
  18.5 159.2 %while.77 = (s32[]{:T(128)}, bf16[2,128,128]{2,1,0:T(8,128)(2,1)S(1)}, f32[2,128,128]{2,1,0:T(8,128)S(1)}, f32[128,4,128]{2,0,1:T(8,128)S(1)}, s32[]{:T(128)}, /...) while((s32[]{:T(128)}, ...), condition=%wide.region_12.13_spmd, body=%wide.region_9.12_spmd.sunk | while | flops 84607240 | bytes 4594019 | solution.py:77
  45.2 5.8 collective-permute-done.2
  54.8 5.8 collective-permute-done.2
  65.7 4.6 collective-permute-done.2
  112.4 4.5 collective-permute-start.3
  134.2 4.5 collective-permute-start.3
  155.9 4.5 collective-permute-start.3
  179.6 43.2 %while.76 = (s32[]{:T(128)}, bf16[2,128,128]{2,1,0:T(8,128)(2,1)S(1)}, f32[2,128,128]{2,1,0:T(8,128)S(1)}, f32[128,4,128]{2,0,1:T(8,128)S(1)}, s32[]{:T(128)}, /...) while((s32[]{:T(128)}, ...), condition=%wide.region_6.7_spmd, body=%wide.region_3.6_spmd.sunk | while | flops 84607240 | bytes 4594019 | solution.py:77
  179.6 4.5 collective-permute-start.1
  224.7 344.5 %while.78 = (s32[]{:T(128)}, bf16[2,128,128]{2,1,0:T(8,128)(2,1)S(1)}, f32[2,128,128]{2,1,0:T(8,128)S(1)}, f32[128,4,128]{2,0,1:T(8,128)S(1)}, s32[]{:T(128)}, /...) while((s32[]{:T(128)}, ...), condition=%wide.region_18.19_spmd, body=%wide.region_15.18_spmd.sunk | while | flops 84607240 | bytes 4594019 | solution.py:77
  235.6 4.5 collective-permute-start.5
  257.5 4.5 collective-permute-start.5
  268.4 4.5 collective-permute-start.5
  279.3 4.5 collective-permute-start.5
  290.3 4.5 collective-permute-start.5
  301.2 4.5 collective-permute-start.5
  312.1 4.5 collective-permute-start.5
  323.1 4.5 collective-permute-start.5
  334.0 4.5 collective-permute-start.5
  344.9 4.5 collective-permute-start.5
  355.9 4.5 collective-permute-start.5
  366.8 4.5 collective-permute-start.5
  377.7 4.5 collective-permute-start.5
  388.7 4.5 collective-permute-start.5
  399.6 4.5 collective-permute-start.5
  410.5 4.5 collective-permute-start.5
  421.4 4.5 collective-permute-start.5
  432.4 4.5 collective-permute-start.5
  443.3 4.5 collective-permute-start.5
  465.2 4.5 collective-permute-start.5
  476.1 4.5 collective-permute-start.5
  498.0 4.5 collective-permute-start.5
  507.1 6.2 collective-permute-start.5
  518.1 4.5 collective-permute-start.5
  522.5 5.0 collective-permute-start.4
  529.0 4.5 collective-permute-start.5
  538.2 6.2 collective-permute-start.5
  549.1 4.5 collective-permute-start.5
  553.6 5.0 collective-permute-start.4
  560.0 4.5 collective-permute-start.5
  571.3 638.0 %while.79 = (s32[]{:T(128)}, bf16[2,128,128]{2,1,0:T(8,128)(2,1)S(1)}, f32[2,128,128]{2,1,0:T(8,128)S(1)}, f32[128,4,128]{2,0,1:T(8,128)S(1)}, s32[]{:T(128)}, /...) while((s32[]{:T(128)}, ...), condition=%wide.region_24.25_spmd, body=%wide.region_21.24_spmd.sunk | while | flops 84607240 | bytes 4594019 | solution.py:77
  571.3 6.2 collective-permute-start.7
  584.0 4.5 collective-permute-start.7
  588.4 5.0 collective-permute-start.6
  607.5 6.2 collective-permute-start.7
  620.1 4.5 collective-permute-start.7
  641.9 4.5 collective-permute-start.7
  663.7 4.5 collective-permute-start.7
  685.4 4.5 collective-permute-start.7
  707.2 4.5 collective-permute-start.7
  729.0 4.5 collective-permute-start.7
  750.7 4.5 collective-permute-start.7
  772.5 4.5 collective-permute-start.7
  794.3 4.5 collective-permute-start.7
  816.0 4.5 collective-permute-start.7
  837.8 4.5 collective-permute-start.7
  857.9 6.2 collective-permute-start.7
  873.2 4.9 collective-permute-start.6
  888.8 6.2 collective-permute-start.7
  904.2 4.9 collective-permute-start.6
  919.8 6.2 collective-permute-start.7
  935.1 4.9 collective-permute-start.6
  941.5 4.5 collective-permute-start.7
  950.7 6.2 collective-permute-start.7
  (1612 shorter events, 1032.5 us)
Async XLA Ops:
  112.4 10.8 collective-permute-start.3
  134.2 10.8 collective-permute-start.3
  155.9 10.8 collective-permute-start.3
  177.7 1036.4 %collective-permute-start.9 = (bf16[2,128,128]{2,1,0:T(8,128)(2,1)S(1)}, bf16[2,128,128]{2,1,0:T(8,128)(2,1)S(1)}, u32[]{:S(2)}, u32[]{:S(2)}) collective-permute-start(bf16[2,128,128]{2,1,0:T(8,128)(2,1)S(1)} %convert_element_type.186), channel_id=1, source_target_pairs={{0,192},{4,196},{8,200},{12,204},{16,208},{20,212},{24,216},{28,22... | collective-permute-start | bytes 196616 | tf_op jit(solution)/shard_map/ppermute | solution.py:21
  222.8 991.2 %collective-permute-start.8 = (bf16[2,128,128]{2,1,0:T(8,128)(2,1)S(1)}, bf16[2,128,128]{2,1,0:T(8,128)(2,1)S(1)}, u32[]{:S(2)}, u32[]{:S(2)}) collective-permute-start(bf16[2,128,128]{2,1,0:T(8,128)(2,1)S(1)} %convert_element_type.184), channel_id=1, source_target_pairs={{0,240},{4,244},{8,248},{12,252},{16,0},{20,4},{24,8},{28,12},{32,... | collective-permute-start | bytes 196616 | tf_op jit(solution)/shard_map/ppermute | solution.py:21
  224.7 10.9 collective-permute-start.5
  235.6 10.9 collective-permute-start.5
  246.6 10.9 collective-permute-start.5
  257.5 10.9 collective-permute-start.5
  268.4 10.9 collective-permute-start.5
  279.3 10.9 collective-permute-start.5
  290.3 10.9 collective-permute-start.5
  301.2 10.9 collective-permute-start.5
  312.1 10.9 collective-permute-start.5
  323.1 10.9 collective-permute-start.5
  334.0 10.9 collective-permute-start.5
  344.9 10.9 collective-permute-start.5
  355.9 10.9 collective-permute-start.5
  366.8 10.9 collective-permute-start.5
  377.7 10.9 collective-permute-start.5
  388.7 10.9 collective-permute-start.5
  399.6 10.9 collective-permute-start.5
  410.5 10.9 collective-permute-start.5
  421.4 10.9 collective-permute-start.5
  432.4 10.9 collective-permute-start.5
  443.3 10.9 collective-permute-start.5
  454.2 10.9 collective-permute-start.5
  465.2 10.9 collective-permute-start.5
  476.1 10.9 collective-permute-start.5
  487.0 10.9 collective-permute-start.5
  507.1 10.9 collective-permute-start.5
  518.1 10.9 collective-permute-start.5
  538.2 10.9 collective-permute-start.5
  549.1 10.9 collective-permute-start.5
  569.2 644.9 %collective-permute-start.10 = (bf16[2,128,128]{2,1,0:T(8,128)(2,1)S(1)}, bf16[2,128,128]{2,1,0:T(8,128)(2,1)S(1)}, u32[]{:S(2)}, u32[]{:S(2)}) collective-permute-start(bf16[2,128,128]{2,1,0:T(8,128)(2,1)S(1)} %convert_element_type.188), channel_id=1, source_target_pairs={{0,128},{4,132},{8,136},{12,140},{16,144},{20,148},{24,152},{28,15... | collective-permute-start | bytes 196616 | tf_op jit(solution)/shard_map/ppermute | solution.py:21
  571.3 12.6 %collective-permute-start.7 = (f32[2,128,128]{2,1,0:T(8,128)S(1)}, f32[2,128,128]{2,1,0:T(8,128)S(1)}, u32[]{:S(2)}, u32[]{:S(2)}) collective-permute-start(f32[2,128,128]{2,1,0:T(8,128)S(1)} %get-tuple-element.1895), channel_id=1, source_target_pairs={{0,4},{4,8},{8,12},{12,16},{16,20},{20,24},{24,28},{28,32},{32,36}... | collective-permute-start | bytes 393224 | tf_op jit(solution)/shard_map/while/body/eval_jaxpr/ppermute | solution.py:21
  584.0 12.6 %collective-permute-start.7 = (f32[2,128,128]{2,1,0:T(8,128)S(1)}, f32[2,128,128]{2,1,0:T(8,128)S(1)}, u32[]{:S(2)}, u32[]{:S(2)}) collective-permute-start(f32[2,128,128]{2,1,0:T(8,128)S(1)} %get-tuple-element.1895), channel_id=1, source_target_pairs={{0,4},{4,8},{8,12},{12,16},{16,20},{20,24},{24,28},{28,32},{32,36}... | collective-permute-start | bytes 393224 | tf_op jit(solution)/shard_map/while/body/eval_jaxpr/ppermute | solution.py:21
  596.6 10.8 collective-permute-start.7
  607.5 12.6 %collective-permute-start.7 = (f32[2,128,128]{2,1,0:T(8,128)S(1)}, f32[2,128,128]{2,1,0:T(8,128)S(1)}, u32[]{:S(2)}, u32[]{:S(2)}) collective-permute-start(f32[2,128,128]{2,1,0:T(8,128)S(1)} %get-tuple-element.1895), channel_id=1, source_target_pairs={{0,4},{4,8},{8,12},{12,16},{16,20},{20,24},{24,28},{28,32},{32,36}... | collective-permute-start | bytes 393224 | tf_op jit(solution)/shard_map/while/body/eval_jaxpr/ppermute | solution.py:21
  620.1 10.8 collective-permute-start.7
  631.0 10.8 collective-permute-start.7
  641.9 10.8 collective-permute-start.7
  652.8 10.8 collective-permute-start.7
  663.7 10.8 collective-permute-start.7
  674.5 10.8 collective-permute-start.7
  685.4 10.8 collective-permute-start.7
  696.3 10.8 collective-permute-start.7
  707.2 10.8 collective-permute-start.7
  718.1 10.8 collective-permute-start.7
  729.0 10.8 collective-permute-start.7
  739.8 10.8 collective-permute-start.7
  750.7 10.8 collective-permute-start.7
  761.6 10.8 collective-permute-start.7
  772.5 10.8 collective-permute-start.7
  794.3 10.8 collective-permute-start.7
  816.0 10.8 collective-permute-start.7
  837.8 10.8 collective-permute-start.7
  857.9 10.8 collective-permute-start.7
  868.8 10.8 collective-permute-start.7
  888.8 10.8 collective-permute-start.7
  899.7 10.8 collective-permute-start.7
  919.8 10.8 collective-permute-start.7
  930.6 10.8 collective-permute-start.7
  950.7 10.8 collective-permute-start.7
  (178 other events, 1070.2 us)
where the time goes:
time: 1240 us; the launch traced here: 1220 us
  starting transfers between devices  879 us (71%)
  waiting for transfers between devices  169 us (14%)
  matrix products  71.1 us (6%)
  other arithmetic  66.3 us (5%)
    ppermute x119, starting transfers between devices, shifted_2(): return lax.ppermute(x, axis, [(i, (i + by) % count) for i in range(count)])  506 us
    ppermute x115, starting transfers between devices, shifted(): lax.ppermute(value, axis, [(source, source + steps) for source in range(i...  373 us
    ppermute x115, waiting for transfers between devices, shifted(): lax.ppermute(value, axis, [(source, source + steps) for source in range(i...  168 us
    and x71, other arithmetic, score_grads(): allowed = (distance >= 0) & (distance < span_value)  54.4 us
  transfers between devices with their start and end apart: 234, of which 116 were waited for; matrix products, arithmetic and copies ran while one was open for 11% of the time, Pallas kernels for 0%

commit v1 on v0

v1 whole, which is shorter than its diff:
```python
import functools
import math

import jax
import jax.numpy as jnp
from jax import lax
from jax.experimental import pallas as pl
from jax.experimental.pallas import tpu as pltpu
from jax.sharding import PartitionSpec as P

Q_HEADS = 16
KV_HEADS = 4
GROUP = 4
HEAD_DIM = 128
PLANES = 8
COLUMNS = 4
ROWS = 128
SCALING = 1.0 / math.sqrt(HEAD_DIM)
LOG2E = math.log2(math.e)
BF16 = jnp.bfloat16
F32 = jnp.float32
MESH = pl.DeviceIdType.MESH
NT = (((1,), (1,)), ((), ()))
NN = (((1,), (0,)), ((), ()))
FAR = ((7, 1), (4, 2))


def dot(a, b, dims=NN):
    return lax.dot_general(a, b, dims, preferred_element_type=F32)


def far_of(core, slot):
    return jnp.where(core == 0, FAR[0][slot], FAR[1][slot])


def pack_kernel(heads, q_ref, g_ref, o_ref, k_ref, v_ref, lse_ref, qd_ref, kv_ref, st_ref):
    head = heads[pl.program_id(0) * 2 + pl.program_id(1)]
    st_ref[0, 0] = jnp.zeros((8, 256), F32)
    for g in range(GROUP):
        cols = slice(g * HEAD_DIM, (g + 1) * HEAD_DIM)
        qd_ref[0, 0, 0, g] = q_ref[:, cols]
        qd_ref[0, 0, 1, g] = g_ref[:, cols]
        product = g_ref[:, cols].astype(F32) * o_ref[:, cols].astype(F32)
        delta = jnp.sum(product.T, axis=0, keepdims=True)
        lanes = slice((g % 2) * ROWS, (g % 2 + 1) * ROWS)
        lse = lse_ref[pl.ds(head * GROUP + g, 1), :]
        st_ref[0, 0, g // 2 : g // 2 + 1, lanes] = lse * LOG2E
        st_ref[0, 0, 2 + g // 2 : 3 + g // 2, lanes] = delta
    kv_ref[0, 0, 0] = k_ref[...]
    kv_ref[0, 0, 1] = v_ref[...]


def pack(heads, queries, out_grad, outputs, keys, values, log_sum_exp):
    wide = pl.BlockSpec((ROWS, GROUP * HEAD_DIM), lambda r, s, h: (0, h[r * 2 + s]))
    narrow = pl.BlockSpec((ROWS, HEAD_DIM), lambda r, s, h: (0, h[r * 2 + s]))
    return pl.pallas_call(
        pack_kernel,
        grid_spec=pltpu.PrefetchScalarGridSpec(
            num_scalar_prefetch=1,
            grid=(2, 2),
            in_specs=[wide, wide, wide, narrow, narrow, pl.BlockSpec((Q_HEADS, ROWS), lambda r, s, h: (0, 0))],
            out_specs=[
                pl.BlockSpec((1, 1, 2, GROUP, ROWS, HEAD_DIM), lambda r, s, h: (r, s, 0, 0, 0, 0)),
                pl.BlockSpec((1, 1, 2, ROWS, HEAD_DIM), lambda r, s, h: (r, s, 0, 0, 0)),
                pl.BlockSpec((1, 1, 8, 256), lambda r, s, h: (r, s, 0, 0)),
            ],
        ),
        out_shape=[
            jax.ShapeDtypeStruct((2, 2, 2, GROUP, ROWS, HEAD_DIM), BF16),
            jax.ShapeDtypeStruct((2, 2, 2, ROWS, HEAD_DIM), BF16),
            jax.ShapeDtypeStruct((2, 2, 8, 256), F32),
        ],
        name="pack",
    )(heads, queries, out_grad, outputs, keys, values, log_sum_exp)


def place():
    me = lax.axis_index("ctx")
    return me // 8, (me // 2) % 4, me % 2


def at(z, y, core):
    return {"ctx": z * 8 + y * 2 + core}


def remote(src, dst, send, recv, device):
    return pltpu.make_async_remote_copy(
        src_ref=src, dst_ref=dst, send_sem=send, recv_sem=recv, device_id=device, device_id_type=MESH
    )


def greet(z, y, core):
    barrier = pltpu.get_barrier_semaphore()
    count = 1
    pl.semaphore_signal(barrier, inc=1, device_id=at(z, y, 1 - core), device_id_type=MESH)
    for c in range(2):
        for dy in range(1, COLUMNS):
            pl.semaphore_signal(barrier, inc=1, device_id=at(z, (y + dy) % 4, c), device_id_type=MESH)
            count += 1
        for dz in range(1, PLANES):
            pl.semaphore_signal(barrier, inc=1, device_id=at((z + dz) % 8, y, c), device_id_type=MESH)
            count += 1
    pl.semaphore_wait(barrier, count)


def spread_kernel(qd_ref, kv_ref, st_ref, qd_all, kv_all, st_all, local, s_sib, s_y, s_fw, s_z, r_q, r_s, r_kv):
    z, y, core = place()
    greet(z, y, core)
    other = 1 - core
    mine = [
        pltpu.make_async_copy(qd_ref.at[0], qd_all.at[y, core], local.at[0]),
        pltpu.make_async_copy(st_ref.at[0], st_all.at[y, core], local.at[1]),
        pltpu.make_async_copy(kv_ref.at[0], kv_all.at[0, core], local.at[2]),
    ]
    for c in mine:
        c.start()
    sends = []
    for role in range(2):
        target = core if role == 0 else other
        for step, dy in enumerate((1, 3)):
            to = at(z, (y + dy) % 4, target)
            for slot in range(2):
                sends.append(
                    remote(
                        qd_ref.at[role, slot],
                        qd_all.at[y, core, slot],
                        s_y.at[role, step, slot],
                        r_q.at[y, core, slot],
                        to,
                    )
                )
            sends.append(remote(st_ref.at[role], st_all.at[y, core], s_y.at[role, step, 2], r_s.at[y, core], to))
    to = at(z, y, other)
    for slot in range(2):
        sends.append(remote(qd_ref.at[1, slot], qd_all.at[y, core, slot], s_sib.at[slot], r_q.at[y, core, slot], to))
        sends.append(
            remote(kv_ref.at[1, slot], kv_all.at[0, core, slot], s_sib.at[2 + slot], r_kv.at[0, core, slot], to)
        )
    sends.append(remote(st_ref.at[1], st_all.at[y, core], s_sib.at[4], r_s.at[y, core], to))
    for c in sends:
        c.start()

    def keys_to(d, slot, role):
        target = core if role == 0 else other
        return remote(
            kv_ref.at[role, slot],
            kv_all.at[d, core, slot],
            s_z.at[d, role, slot],
            r_kv.at[d, core, slot],
            at((z + d) % 8, y, target),
        )

    def each_key_send(act):
        for d in range(1, PLANES):
            for role in range(2):
                target = core if role == 0 else other
                for slot in range(2):
                    if d <= max(FAR[0][slot], FAR[1][slot]):

                        @pl.when((z + d < PLANES) & (d <= far_of(target, slot)))
                        def _(d=d, slot=slot, role=role):
                            act(keys_to(d, slot, role))

    each_key_send(lambda c: c.start())

    def landed(col, c, slot):
        return remote(qd_ref.at[0, slot], qd_all.at[col, c, slot], s_sib.at[0], r_q.at[col, c, slot], to)

    def landed_st(col, c):
        return remote(st_ref.at[0], st_all.at[col, c], s_sib.at[0], r_s.at[col, c], to)

    forwards = []
    before, after, across = (y + 3) % 4, (y + 1) % 4, (y + 2) % 4
    for c in range(2):
        landed(before, c, 0).wait_recv()
        landed_st(before, c).wait_recv()
        up = at(z, after, core)
        forwards.append(
            remote(qd_all.at[before, c, 0], qd_all.at[before, c, 0], s_fw.at[c, 0], r_q.at[before, c, 0], up)
        )
        forwards.append(remote(st_all.at[before, c], st_all.at[before, c], s_fw.at[c, 1], r_s.at[before, c], up))
        forwards[-2].start()
        forwards[-1].start()
        landed(after, c, 1).wait_recv()
        down = at(z, before, core)
        forwards.append(
            remote(qd_all.at[after, c, 1], qd_all.at[after, c, 1], s_fw.at[c, 2], r_q.at[after, c, 1], down)
        )
        forwards[-1].start()
    for c in range(2):
        landed(before, c, 1).wait_recv()
        landed(after, c, 0).wait_recv()
        landed_st(after, c).wait_recv()
        landed(across, c, 0).wait_recv()
        landed(across, c, 1).wait_recv()
        landed_st(across, c).wait_recv()
    for slot in range(2):
        landed(y, other, slot).wait_recv()
    landed_st(y, other).wait_recv()

    def keys_landed(d, c, slot):
        return remote(kv_ref.at[0, slot], kv_all.at[d, c, slot], s_sib.at[0], r_kv.at[d, c, slot], to)

    for slot in range(2):
        keys_landed(0, other, slot).wait_recv()
        for d in range(1, max(FAR[0][slot], FAR[1][slot]) + 1):

            @pl.when((z >= d) & (d <= far_of(core, slot)))
            def _(d=d, slot=slot):
                for c in range(2):
                    keys_landed(d, c, slot).wait_recv()

    for c in mine:
        c.wait()
    for c in sends + forwards:
        c.wait_send()
    each_key_send(lambda c: c.wait_send())


def spread(qd, kv, st):
    anywhere = pl.BlockSpec(memory_space=pl.ANY)
    dma = pltpu.SemaphoreType.DMA
    return pl.pallas_call(
        spread_kernel,
        in_specs=[anywhere] * 3,
        out_specs=[anywhere] * 3,
        out_shape=[
            jax.ShapeDtypeStruct((COLUMNS, 2, 2, 2, GROUP, ROWS, HEAD_DIM), BF16),
            jax.ShapeDtypeStruct((PLANES, 2, 2, 2, ROWS, HEAD_DIM), BF16),
            jax.ShapeDtypeStruct((COLUMNS, 2, 2, 8, 256), F32),
        ],
        scratch_shapes=[
            dma((3,)),
            dma((5,)),
            dma((2, 2, 3)),
            dma((2, 3)),
            dma((PLANES, 2, 2)),
            dma((COLUMNS, 2, 2)),
            dma((COLUMNS, 2)),
            dma((PLANES, 2, 2)),
        ],
        compiler_params=pltpu.CompilerParams(collective_id=0, has_side_effects=True),
        name="spread",
    )(qd, kv, st)


def grads_kernel(info, qd_ref, kv_ref, st_ref, dq_ref, dkv_ref, dq_acc, dkv_acc):
    z, y = info[0], info[1]
    dkv_acc[...] = jnp.zeros_like(dkv_acc)

    def tile(slot, col, d0, count, span, masked):
        size = count * 256
        k = kv_ref[pl.ds(d0, count), :, slot, 0].reshape(size, HEAD_DIM)
        v = kv_ref[pl.ds(d0, count), :, slot, 1].reshape(size, HEAD_DIM)
        k_t = k.T
        for half in range(2):
            for pair in range(2):
                heads = slice(2 * pair, 2 * pair + 2)
                q = qd_ref[col, half, slot, 0, heads].reshape(256, HEAD_DIM)
                g = qd_ref[col, half, slot, 1, heads].reshape(256, HEAD_DIM)
                lse = st_ref[col, half, slot, pair : pair + 1]
                delta = st_ref[col, half, slot, 2 + pair : 3 + pair]
                prob = jnp.exp2(dot(k, q, NT) * (SCALING * LOG2E) - lse)
                if masked:
                    key = lax.broadcasted_iota(jnp.int32, (size, 256), 0)
                    row = lax.broadcasted_iota(jnp.int32, (size, 256), 1) % ROWS
                    distance = row - key + (d0 * 1024 + (col - y) * 256 + half * ROWS)
                    prob = jnp.where((distance >= 0) & (distance < span), prob, 0.0)
                ds = (prob * (dot(v, g, NT) - delta)).astype(BF16)
                low = prob.astype(BF16)
                dkv_acc[slot, 0, pl.ds(d0, count)] += dot(ds, q).reshape(count, 256, HEAD_DIM)
                dkv_acc[slot, 1, pl.ds(d0, count)] += dot(low, g).reshape(count, 256, HEAD_DIM)
                dq_acc[half, pair] += dot(k_t, ds)

    for slot in range(2):
        span = info[2 + slot]

        def column(col, carry, slot=slot, span=span):
            dq_acc[...] = jnp.zeros_like(dq_acc)
            ahead = col - y
            low = jnp.where(ahead >= 0, 0, 1)
            high = jnp.minimum(z, ((span + 254) // 256 - ahead + 4) // 4 - 1)
            full_low = jnp.where(ahead > 0, 0, 1)
            full_high = jnp.minimum(z, ((span - 256) // 256 - ahead + 4) // 4 - 1)
            full_count = jnp.maximum(full_high - full_low + 1, 0)

            def edge(d, c):
                tile(slot, col, d, 1, span, True)
                return c

            lax.fori_loop(low, jnp.minimum(full_low, high + 1), edge, 0)
            lax.fori_loop(jnp.maximum(full_low + full_count, low), high + 1, edge, 0)
            fours = full_count // 4

            def four(i, c):
                tile(slot, col, full_low + 4 * i, 4, span, False)
                return c

            lax.fori_loop(0, fours, four, 0)
            rest = full_count - 4 * fours
            start = full_low + 4 * fours

            def two(i, c):
                tile(slot, col, start, 2, span, False)
                return c

            lax.fori_loop(0, rest // 2, two, 0)

            def one(i, c):
                tile(slot, col, full_low + full_count - 1, 1, span, False)
                return c

            lax.fori_loop(0, rest % 2, one, 0)
            for half in range(2):
                for pair in range(2):
                    total = dq_acc[half, pair].T * SCALING
                    dq_ref[col, half, slot, 2 * pair : 2 * pair + 2] = total.reshape(2, ROWS, HEAD_DIM).astype(BF16)
            return carry

        lax.fori_loop(0, COLUMNS, column, 0)

    def finish(d, c):
        for slot in range(2):
            for half in range(2):
                rows = slice(half * ROWS, (half + 1) * ROWS)
                dkv_ref[d, half, slot, 0] = (dkv_acc[slot, 0, d, rows] * SCALING).astype(BF16)
                dkv_ref[d, half, slot, 1] = dkv_acc[slot, 1, d, rows].astype(BF16)
        return c

    lax.fori_loop(0, PLANES, finish, 0)


def grads(info, qd_all, kv_all, st_all):
    whole = pl.BlockSpec(memory_space=pltpu.VMEM)
    return pl.pallas_call(
        grads_kernel,
        in_specs=[pl.BlockSpec(memory_space=pltpu.SMEM), whole, whole, whole],
        out_specs=[whole, whole],
        out_shape=[
            jax.ShapeDtypeStruct((COLUMNS, 2, 2, GROUP, ROWS, HEAD_DIM), BF16),
            jax.ShapeDtypeStruct((PLANES, 2, 2, 2, ROWS, HEAD_DIM), BF16),
        ],
        scratch_shapes=[
            pltpu.VMEM((2, 2, HEAD_DIM, 256), F32),
            pltpu.VMEM((2, 2, PLANES, 256, HEAD_DIM), F32),
        ],
        compiler_params=pltpu.CompilerParams(vmem_limit_bytes=56 * 2**20),
        name="grads",
    )(info, qd_all, kv_all, st_all)


def collect_kernel(dq_ref, dkv_ref, rq, rkv, local, s_q, s_kv, r_q, r_kv):
    z, y, core = place()
    greet(z, y, core)
    other = 1 - core
    mine = [
        pltpu.make_async_copy(dq_ref.at[y, core], rq.at[y, core], local.at[0]),
        pltpu.make_async_copy(dkv_ref.at[0, core], rkv.at[0, core], local.at[1]),
    ]
    for c in mine:
        c.start()

    def query_send(dy, half):
        col = (y + dy) % 4
        return remote(dq_ref.at[col, half], rq.at[y, core], s_q.at[dy, half], r_q.at[y, core], at(z, col, half))

    def key_send(d, half, slot):
        return remote(
            dkv_ref.at[d, half, slot],
            rkv.at[d, core, slot],
            s_kv.at[d, half, slot],
            r_kv.at[d, core, slot],
            at((z + 8 - d) % 8, y, half),
        )

    def each_key_send(act):
        for d in range(PLANES - 1, 0, -1):
            for slot in range(2):
                if d <= max(FAR[0][slot], FAR[1][slot]):

                    @pl.when((z >= d) & (d <= far_of(core, slot)))
                    def _(d=d, slot=slot):
                        for half in range(2):
                            act(key_send(d, half, slot))

    sends = [query_send(dy, half) for dy in (2, 1, 3) for half in range(2)]
    sends.append(remote(dq_ref.at[y, other], rq.at[y, core], s_q.at[0, 0], r_q.at[y, core], at(z, y, other)))
    for slot in range(2):
        sends.append(
            remote(
                dkv_ref.at[0, other, slot],
                rkv.at[0, core, slot],
                s_kv.at[0, 0, slot],
                r_kv.at[0, core, slot],
                at(z, y, other),
            )
        )
    for c in sends:
        c.start()
    each_key_send(lambda c: c.start())

    to = at(z, y, other)

    def query_landed(col, c):
        return remote(dq_ref.at[0, 0], rq.at[col, c], s_q.at[0, 0], r_q.at[col, c], to)

    def key_landed(d, c, slot):
        return remote(dkv_ref.at[0, 0, slot], rkv.at[d, c, slot], s_kv.at[0, 0, slot], r_kv.at[d, c, slot], to)

    query_landed(y, other).wait_recv()
    for dy in range(1, COLUMNS):
        for c in range(2):
            query_landed((y + dy) % 4, c).wait_recv()
    for slot in range(2):
        key_landed(0, other, slot).wait_recv()
        for d in range(1, PLANES):
            for c in range(2):
                if d <= FAR[c][slot]:

                    @pl.when(z + d < PLANES)
                    def _(d=d, slot=slot, c=c):
                        key_landed(d, c, slot).wait_recv()

    for c in mine:
        c.wait()
    for c in sends:
        c.wait_send()
    each_key_send(lambda c: c.wait_send())


def collect(dq, dkv):
    anywhere = pl.BlockSpec(memory_space=pl.ANY)
    dma = pltpu.SemaphoreType.DMA
    return pl.pallas_call(
        collect_kernel,
        in_specs=[anywhere] * 2,
        out_specs=[anywhere] * 2,
        out_shape=[
            jax.ShapeDtypeStruct((COLUMNS, 2, 2, GROUP, ROWS, HEAD_DIM), BF16),
            jax.ShapeDtypeStruct((PLANES, 2, 2, 2, ROWS, HEAD_DIM), BF16),
        ],
        scratch_shapes=[
            dma((2,)),
            dma((COLUMNS, 2)),
            dma((PLANES, 2, 2)),
            dma((COLUMNS, 2)),
            dma((PLANES, 2, 2)),
        ],
        compiler_params=pltpu.CompilerParams(collective_id=1, has_side_effects=True),
        name="collect",
    )(dq, dkv)


def finish_kernel(info, rq_ref, rkv_ref, dq_ref, dk_ref, dv_ref):
    core, slot = pl.program_id(0), pl.program_id(1)
    for g in range(GROUP):
        total = rq_ref[0, 0, 0, g].astype(F32)
        for col in range(1, COLUMNS):
            total += rq_ref[col, 0, 0, g].astype(F32)
        dq_ref[:, g * HEAD_DIM : (g + 1) * HEAD_DIM] = total.astype(BF16)
    far = jnp.where(
        core == 0, jnp.where(slot == 0, FAR[0][0], FAR[0][1]), jnp.where(slot == 0, FAR[1][0], FAR[1][1])
    )
    last = jnp.minimum(far, PLANES - 1 - info[4])

    def add(d, carry):
        return carry[0] + rkv_ref[d, 0, 0, 0].astype(F32), carry[1] + rkv_ref[d, 0, 0, 1].astype(F32)

    dk, dv = lax.fori_loop(
        1, last + 1, add, (rkv_ref[0, 0, 0, 0].astype(F32), rkv_ref[0, 0, 0, 1].astype(F32))
    )
    dk_ref[...] = dk.astype(BF16)
    dv_ref[...] = dv.astype(BF16)


def finish(info, rq, rkv):
    return pl.pallas_call(
        finish_kernel,
        grid_spec=pltpu.PrefetchScalarGridSpec(
            num_scalar_prefetch=1,
            grid=(2, 2),
            in_specs=[
                pl.BlockSpec((COLUMNS, 1, 1, GROUP, ROWS, HEAD_DIM), lambda c, s, h: (0, c, s, 0, 0, 0)),
                pl.BlockSpec((PLANES, 1, 1, 2, ROWS, HEAD_DIM), lambda c, s, h: (0, c, s, 0, 0, 0)),
            ],
            out_specs=[
                pl.BlockSpec((ROWS, GROUP * HEAD_DIM), lambda c, s, h: (0, h[c * 2 + s])),
                pl.BlockSpec((ROWS, HEAD_DIM), lambda c, s, h: (0, h[c * 2 + s])),
                pl.BlockSpec((ROWS, HEAD_DIM), lambda c, s, h: (0, h[c * 2 + s])),
            ],
        ),
        out_shape=[
            jax.ShapeDtypeStruct((ROWS, Q_HEADS * HEAD_DIM), BF16),
            jax.ShapeDtypeStruct((ROWS, KV_HEADS * HEAD_DIM), BF16),
            jax.ShapeDtypeStruct((ROWS, KV_HEADS * HEAD_DIM), BF16),
        ],
        name="finish",
    )(info, rq, rkv)


def per_device(queries, keys, values, outputs, out_grad, log_sum_exp, spans):
    z, y, core = place()
    sequence = ROWS * lax.axis_size("ctx")
    numbers = jnp.arange(KV_HEADS, dtype=jnp.int32)

    def head_of(low, top):
        return jnp.sum(jnp.where((spans > low) & (spans <= top), numbers, 0))

    short = head_of(0, sequence // 16)
    middle = head_of(sequence // 8, sequence // 4)
    half = head_of(sequence // 4, sequence // 2)
    whole = head_of(sequence // 2, sequence)
    ordered = jnp.stack([whole, short, half, middle]).astype(jnp.int32)
    swapped = jnp.stack([half, middle, whole, short]).astype(jnp.int32)
    heads = jnp.where(core == 0, ordered, swapped)
    own_spans = jnp.stack(
        [jnp.sum(jnp.where(numbers == heads[slot], spans, 0)).astype(jnp.int32) for slot in range(2)]
    )
    info = jnp.concatenate([jnp.stack([z, y]).astype(jnp.int32), own_spans])
    qd, kv, st = pack(heads, queries, out_grad, outputs, keys, values, log_sum_exp)
    qd_all, kv_all, st_all = spread(qd, kv, st)
    dq, dkv = grads(info, qd_all, kv_all, st_all)
    rq, rkv = collect(dq, dkv)
    return tuple(finish(jnp.concatenate([ordered, jnp.stack([z]).astype(jnp.int32)]), rq, rkv))


def solution(mesh):
    in_specs = (
        P(("dp", "ctx"), None),
        P(("dp", "ctx"), None),
        P(("dp", "ctx"), None),
        P(("dp", "ctx"), None),
        P(("dp", "ctx"), None),
        P(None, ("dp", "ctx")),
        P("dp"),
    )
    out_specs = (P(("dp", "ctx"), None), P(("dp", "ctx"), None), P(("dp", "ctx"), None))
    return jax.shard_map(
        per_device, mesh=mesh, in_specs=in_specs, out_specs=out_specs, check_vma=False
    )
```

time: 1240 us -> 132 us (0.11); the launches traced: 1220 us -> 131 us
  starting transfers between devices: 879 us -> 0 us
  waiting for transfers between devices: 169 us -> 0 us
  Pallas kernels: 0 us -> 118 us
  matrix products: 71.1 us -> 0 us
  other arithmetic: 66.3 us -> 8.56 us
    ppermute x234 -> x0, starting transfers between devices: 879 us -> none  [the longest x119 506 us: shifted_2(): return lax.ppermute(x, axis, [(i, (i + by) % count) for i in range(count)])]
    ppermute x234 -> x0, waiting for transfers between devices: 169 us -> none  [the longest x115 168 us: shifted(): lax.ppermute(value, axis, [(source, source + steps) for source in range(i...]
    pallas_call x0 -> x5, Pallas kernels: none -> 118 us  [the longest x1 45.2 us: spread(): pl.pallas_call(spread_kernel, in_specs=[anywhere] * 3, out_specs=[anywher...]
    dot_general x370 -> x0, matrix products: 71.1 us -> none  [the longest x74 15.5 us: query_part(): jnp.einsum('gts,sd->tgd', dscores, key_rows, preferred_element_type=jnp.f...]
    and x71 -> x0, other arithmetic: 54.4 us -> none  [score_grads(): allowed = (distance >= 0) & (distance < span_value)]
  transfers between devices with their start and end apart: 234 -> 0, of which waited for: 116 -> 0; matrix products, arithmetic and copies ran while one was open for 11% -> 0% of each run, Pallas kernels for 0% -> 0%
where the time goes in v1:
time: 132 us; the launch traced here: 131 us
  Pallas kernels  118 us (89%)
  other arithmetic  8.56 us (6%)
  local copies, waits for them, and re-layouts  3.84 us (3%)
    pallas_call x1, Pallas kernels, spread(): pl.pallas_call(spread_kernel, in_specs=[anywhere] * 3, out_specs=[anywher...  45.2 us
    pallas_call x1, Pallas kernels, collect(): pl.pallas_call(collect_kernel, in_specs=[anywhere] * 2, out_specs=[anywhe...  34.1 us
    pallas_call x1, Pallas kernels, grads(): pl.pallas_call(grads_kernel, in_specs=[pl.BlockSpec(memory_space=pltpu.SM...  29.5 us
    pallas_call x1, Pallas kernels, finish(): pl.pallas_call(finish_kernel, grid_spec=pltpu.PrefetchScalarGridSpec(num_...  4.79 us
    pallas_call x1, Pallas kernels, pack(): pl.pallas_call(pack_kernel, grid_spec=pltpu.PrefetchScalarGridSpec(num_sc...  4.44 us
    concatenate x1, local copies, waits for them, and re-layouts, per_device(): jnp.concatenate([ordered, jnp.stack([z]).astype(jnp.int32)])  3.25 us
    reduce_sum x1, other arithmetic, per_device(): jnp.sum(jnp.where(numbers == heads[slot], spans, 0)).astype(jnp.int32)  2.65 us
    select_n x1, other arithmetic, per_device(): heads = jnp.where(core == 0, ordered, swapped)  2.64 us

profile of v1, /device:TPU:103, one launch (start us, length us, event | category | flops | bytes accessed | tf_op | source)
XLA Modules:
  0.0 131.2 jit_solution(7345116030700198718)
XLA Ops:
  0.7 1.4 %fusion.2 = (s32[]{:T(128)}, s32[]{:T(128)}, s32[]{:T(128)}, s32[]{:T(128)}) fusion(s32[4]{0:T(128)} %param.13), kind=kLoop, calls=%fused_computation.10 | loop fusion | flops 76 | bytes 32 | tf_op jit(solution)/shard_map/reduce_sum | solution.py:507
  2.1 2.6 %broadcast_select_fusion.heads = s32[4]{0:T(128)S(1)} fusion(pred[]{:T(512)S(6)} %eq.18, s32[1]{0:T(128)} %bitcast.3, s32[1]{0:T(128)} %bitcast.2, s32[1]{0:T(128)} %bitcast.1, s32[1]{0:T(128)} %bitcast), kind=kLoop, calls=%fused_computation.6 | loop fusion | flops 28 | bytes 33 | tf_op jit(solution)/shard_map/jit(_where)/select_n | solution.py:515
  4.7 0.0 copy-start
  4.7 3.3 %concatenate.7.info = s32[5]{0:T(128)} concatenate(s32[1]{0:T(128)} %bitcast, s32[1]{0:T(128)} %bitcast.1, s32[1]{0:T(128)} %bitcast.2, s32[1]{0:T(128)} %bitcast.3, s32[1]{0:T(128)} %bitcast.4), dimensions={0} | concatenate | bytes 40 | tf_op jit(solution)/shard_map/concatenate | solution.py:524
  8.0 0.6 fusion.6
  8.6 2.7 %fusion = (s32[]{:T(128)}, s32[]{:T(128)}) fusion(s32[4]{0:T(128)} %param.13, s32[]{:T(128)} %bitcast.6, s32[]{:T(128)} %bitcast.8), kind=kLoop, calls=%fused_computation.7 | loop fusion | flops 22 | bytes 32 | tf_op jit(solution)/shard_map/reduce_sum | solution.py:517
  11.2 1.9 %pad_add_fusion.info = s32[4]{0:T(128)} fusion(s32[1]{0:T(128)} %bitcast.9, s32[1]{0:T(128)} %bitcast.7, s32[1]{0:T(128)} %bitcast.5, s32[1]{0:T(128)} %bitcast.4), kind=kLoop, calls=%fused_computation.9 | loop fusion | flops 12 | bytes 32 | tf_op jit(solution)/shard_map/concatenate | solution.py:519
  13.1 0.0 copy-done
  13.1 4.4 %pack.1 = (bf16[2,2,2,4,128,128]{5,4,3,2,1,0:T(8,128)(2,1)}, bf16[2,2,2,128,128]{4,3,2,1,0:T(8,128)(2,1)}, f32[2,2,8,256]{3,2,1,0:T(8,128)}) custom-call(s32[4]{0:T(128)} %copy-done, bf16[128,2048]{1,0:T(8,128)(2,1)} %q_ref.1, bf16[128,2048]{1,0:T(8,128)(2,1)} %g_ref.1, bf16[128,2048]{1,0:T(8,128)(2,1)} %o_ref.1, bf16[128,512]{1,0:T(8,128)(2,1)} %k_ref.1, ...), custom_call_target="tpu_custom_call" | custom-call | tf_op jit(solution)/shard_map/pack/pallas_call | solution.py:56
  17.5 45.2 %spread.1 = (bf16[4,2,2,2,4,128,128]{6,5,4,3,2,1,0:T(8,128)(2,1)}, bf16[8,2,2,2,128,128]{5,4,3,2,1,0:T(8,128)(2,1)}, f32[4,2,2,8,256]{4,3,2,1,0:T(8,128)}) custom-call(bf16[2,2,2,4,128,128]{5,4,3,2,1,0:T(8,128)(2,1)} %get-tuple-element.13.qd_ref, bf16[2,2,2,128,128]{4,3,2,1,0:T(8,128)(2,1)} %get-tuple-element.14.kv_ref, ...), custom_call_target="tpu_custom_call" | custom-call | tf_op jit(solution)/shard_map/spread/pallas_call | solution.py:223
  62.8 29.5 %grads.1 = (bf16[4,2,2,4,128,128]{5,4,3,2,1,0:T(8,128)(2,1)}, bf16[8,2,2,2,128,128]{5,4,3,2,1,0:T(8,128)(2,1)}) custom-call(s32[4]{0:T(128)} %pad_add_fusion.info, bf16[4,2,2,2,4,128,128]{6,5,4,3,2,1,0:T(8,128)(2,1)} %get-tuple-element.16.qd_ref, bf16[8,2,2,2,128,128]{5,4,3,2,1,0:T(8,128)(2,1)} %get-tuple-element.17.kv_ref, ...), custom_call_target="tpu_custom_call" | custom-call | tf_op jit(solution)/shard_map/grads/pallas_call | solution.py:335
  92.3 34.1 %collect.1 = (bf16[4,2,2,4,128,128]{5,4,3,2,1,0:T(8,128)(2,1)}, bf16[8,2,2,2,128,128]{5,4,3,2,1,0:T(8,128)(2,1)}) custom-call(bf16[4,2,2,4,128,128]{5,4,3,2,1,0:T(8,128)(2,1)} %get-tuple-element.19.dq_ref, bf16[8,2,2,2,128,128]{5,4,3,2,1,0:T(8,128)(2,1)} %get-tuple-element.20.dkv_ref), custom_call_target="tpu_custom_call" | custom-call | tf_op jit(solution)/shard_map/collect/pallas_call | solution.py:434
  126.4 4.8 %finish.1 = (bf16[128,2048]{1,0:T(8,128)(2,1)}, bf16[128,512]{1,0:T(8,128)(2,1)}, bf16[128,512]{1,0:T(8,128)(2,1)}) custom-call(s32[5]{0:T(128)} %concatenate.7.info, bf16[4,2,2,4,128,128]{5,4,3,2,1,0:T(8,128)(2,1)} %get-tuple-element.21.rq_ref, bf16[8,2,2,2,128,128]{5,4,3,2,1,0:T(8,128)(2,1)} %get-tuple-element.22.rkv_ref), custom_call_target="tpu_custom_call" | custom-call | tf_op jit(solution)/shard_map/finish/pallas_call | solution.py:477
Async XLA Ops:
  4.7 8.4 %copy-start = (s32[4]{0:T(128)}, s32[4]{0:T(128)S(1)}, u32[]{:S(2)}) copy-start(s32[4]{0:T(128)S(1)} %broadcast_select_fusion.heads) | copy-start | bytes 52

commit v2 on v0

v2 whole, which is shorter than its diff:
```python
import functools
import math

import jax
import jax.numpy as jnp
from jax import lax
from jax.experimental import pallas as pl
from jax.experimental.pallas import tpu as pltpu
from jax.sharding import PartitionSpec as P

Q_HEADS = 16
KV_HEADS = 4
GROUP = 4
HEAD_DIM = 128
PLANES = 8
COLUMNS = 4
ROWS = 128
SCALING = 1.0 / math.sqrt(HEAD_DIM)
LOG2E = math.log2(math.e)
BF16 = jnp.bfloat16
F32 = jnp.float32
MESH = pl.DeviceIdType.MESH
NT = (((1,), (1,)), ((), ()))
NN = (((1,), (0,)), ((), ()))
REACH = ((31, 2), (16, 8))
PLAIN = ((31, 0), (7, 3))
UP = ((3, 1), (4, 2))
DOWN = 4


def dot(a, b, dims=NN):
    return lax.dot_general(a, b, dims, preferred_element_type=F32)


def place():
    me = lax.axis_index("ctx")
    return me // 8, (me // 2) % 4, me % 2


def at(z, y, core):
    return {"ctx": z * 8 + y * 2 + core}


def remote(src, dst, send, recv, device):
    return pltpu.make_async_remote_copy(
        src_ref=src, dst_ref=dst, send_sem=send, recv_sem=recv, device_id=device, device_id_type=MESH
    )


def by_class(table, core, slot):
    first, second = table
    low = first[0] + (first[1] - first[0]) * slot
    high = second[0] + (second[1] - second[0]) * slot
    return low + (high - low) * core


def kernel(
    spans_ref,
    q_ref,
    k_ref,
    v_ref,
    o_ref,
    g_ref,
    lse_ref,
    dq_out,
    dk_out,
    dv_out,
    qd,
    kv,
    st,
    q_sib,
    kv_sib,
    st_sib,
    dq_acc,
    dkv_acc,
    dq_part,
    dq_in,
    dkv_send,
    dkv_in,
    fq,
    fkv,
    s_sib,
    r_sib,
    s_q,
    s_st,
    r_q,
    r_st,
    s_fq,
    s_fst,
    s_up,
    s_down,
    r_kv,
    s_dq,
    r_dq,
    s_dup,
    s_ddown,
    r_dkv,
    s_fin,
    r_fin,
):
    z, y, core = place()
    other = 1 - core
    sibling = at(z, y, other)
    before, after, across = (y + 3) % 4, (y + 1) % 4, (y + 2) % 4
    left, right, far = at(z, before, core), at(z, after, core), at(z, across, core)
    above, below = at((z + 1) % 8, y, core), at((z + 7) % 8, y, core)

    barrier = pltpu.get_barrier_semaphore()
    for peer in (sibling, left, right, far, above, below):
        pl.semaphore_signal(barrier, inc=1, device_id=peer, device_id_type=MESH)

    spans = [spans_ref[i] for i in range(KV_HEADS)]
    tops = ((4096, 8192), (0, 512), (2048, 4096), (1024, 2048))
    chosen_of, limits = [], []
    for low, top in tops:
        picks = [jnp.where((span > low) & (span <= top), 1, 0) for span in spans]
        chosen_of.append(picks)
        limits.append(sum(pick * span for pick, span in zip(picks, spans)))

    def pack(picks, q_to, kv_to, st_to):
        weights = [pick.astype(F32) for pick in picks]

        def taken(ref, g, width):
            total = None
            for head in range(KV_HEADS):
                first = head * width + g * HEAD_DIM
                term = ref[:, first : first + HEAD_DIM] * weights[head].astype(BF16)
                total = term if total is None else total + term
            return total

        st_to[...] = jnp.zeros((8, 256), F32)
        for g in range(GROUP):
            grad = taken(g_ref, g, 512)
            q_to[0, g] = taken(q_ref, g, 512)
            q_to[1, g] = grad
            product = grad.astype(F32) * taken(o_ref, g, 512).astype(F32)
            lanes = slice((g % 2) * ROWS, (g % 2 + 1) * ROWS)
            lse = sum(
                lse_ref[head * GROUP + g : head * GROUP + g + 1, :] * weights[head] for head in range(KV_HEADS)
            )
            st_to[g // 2 : g // 2 + 1, lanes] = lse * LOG2E
            st_to[2 + g // 2 : 3 + g // 2, lanes] = jnp.sum(product.T, axis=0, keepdims=True)
        kv_to[0] = taken(k_ref, 0, HEAD_DIM)
        kv_to[1] = taken(v_ref, 0, HEAD_DIM)

    for slot in range(2):
        theirs = [jnp.where(core == 0, a, b) for a, b in zip(chosen_of[2 + slot], chosen_of[slot])]
        pack(theirs, q_sib.at[slot], kv_sib.at[slot], st_sib.at[slot])

    pl.semaphore_wait(barrier, 6)

    sib_copies = [
        remote(kv_sib, kv.at[0, core], s_sib.at[0], r_sib.at[0], sibling),
        remote(q_sib, qd.at[y, core], s_sib.at[1], r_sib.at[1], sibling),
        remote(st_sib, st.at[y, core], s_sib.at[2], r_sib.at[2], sibling),
    ]
    for c in sib_copies:
        c.start()

    for slot in range(2):
        ours = [jnp.where(core == 0, a, b) for a, b in zip(chosen_of[slot], chosen_of[2 + slot])]
        pack(ours, qd.at[y, core, slot], kv.at[0, core, slot], st.at[y, core, slot])

    def q_copy(half, slot, way):
        return remote(
            qd.at[y, half, slot],
            qd.at[y, half, slot],
            s_q.at[half, slot, way],
            r_q.at[y, half, slot],
            right if way == 0 else left,
        )

    def st_copy(half, way):
        return remote(
            st.at[y, half], st.at[y, half], s_st.at[half, way], r_st.at[y, half], right if way == 0 else left
        )

    def start_q(half):
        for way in range(2):
            st_copy(half, way).start()
        for way in range(2):
            q_copy(half, way, way).start()
        for way in range(2):
            q_copy(half, 1 - way, way).start()

    start_q(core)

    def up_copy(d, slot):
        return remote(kv.at[d, :, slot], kv.at[d + 1, :, slot], s_up.at[d, slot], r_kv.at[d + 1, slot], above)

    def down_copy(e):
        return remote(
            kv.at[(8 - e) % 8, :, 0], kv.at[7 - e, :, 0], s_down.at[e], r_kv.at[7 - e, 0], below
        )

    def goes_up(d, slot):
        return (z + 1 < PLANES) & (z >= d) & (d < by_class(UP, core, slot))

    def goes_down(e):
        return (core == 0) & (e < DOWN) & ((z + e) % 8 < DOWN)

    def forward(i):
        for slot in range(2):

            @pl.when(goes_up(i, slot))
            def _(slot=slot):
                up_copy(i, slot).start()

        @pl.when(goes_down(i))
        def _():
            down_copy(i).start()

    def kv_landed(d, slot):
        return remote(kv.at[0, :, 0], kv.at[d, :, slot], s_up.at[0, 0], r_kv.at[d, slot], sibling)

    def arrive(i):
        for slot in range(2):

            @pl.when((z >= i) & (i <= by_class(UP, core, slot)))
            def _(slot=slot):
                kv_landed(i, slot).wait_recv()

        @pl.when((core == 0) & ((z + i) % 8 < DOWN))
        def _():
            kv_landed(8 - i, 0).wait_recv()

    sib_copies[0].wait_recv()
    forward(0)
    sib_copies[1].wait_recv()
    sib_copies[2].wait_recv()
    start_q(other)

    dkv_acc[...] = jnp.zeros_like(dkv_acc)
    own_limits = [jnp.where(core == 0, limits[slot], limits[2 + slot]) for slot in range(2)]

    def tile(slot, col, d0, count, masked):
        size = count * 256
        k = kv[pl.ds(d0, count), :, slot, 0].reshape(size, HEAD_DIM)
        v = kv[pl.ds(d0, count), :, slot, 1].reshape(size, HEAD_DIM)
        k_t = k.T
        for half in range(2):
            for pair in range(2):
                chosen = slice(2 * pair, 2 * pair + 2)
                q = qd[col, half, slot, 0, chosen].reshape(256, HEAD_DIM)
                g = qd[col, half, slot, 1, chosen].reshape(256, HEAD_DIM)
                lse = st[col, half, slot, pair : pair + 1]
                delta = st[col, half, slot, 2 + pair : 3 + pair]
                prob = jnp.exp2(dot(k, q, NT) * (SCALING * LOG2E) - lse)
                if masked:
                    limit = jnp.where(slot == 0, own_limits[0], own_limits[1])
                    key = lax.broadcasted_iota(jnp.int32, (size, 256), 0)
                    row = lax.broadcasted_iota(jnp.int32, (size, 256), 1) % ROWS
                    distance = row - key + (d0 * 1024 + (col - y) * 256 + half * ROWS)
                    prob = jnp.where((distance >= 0) & (distance < limit), prob, 0.0)
                ds = (prob * (dot(v, g, NT) - delta)).astype(BF16)
                low = prob.astype(BF16)
                dkv_acc[slot, 0, pl.ds(d0, count)] += dot(ds, q).reshape(count, 256, HEAD_DIM)
                dkv_acc[slot, 1, pl.ds(d0, count)] += dot(low, g).reshape(count, 256, HEAD_DIM)
                dq_acc[slot, half, pair] += dot(k_t, ds)

    def last_block(table, slot, ahead):
        return jnp.minimum(z, (by_class(table, core, slot) - ahead + 4) // 4 - 1)

    def write_dq(col, slot):
        for half in range(2):
            for pair in range(2):
                total = dq_acc[slot, half, pair].T * SCALING
                dq_part[col, slot, half, 2 * pair : 2 * pair + 2] = total.reshape(2, ROWS, HEAD_DIM).astype(BF16)

    dq_acc[...] = jnp.zeros_like(dq_acc)

    def diagonal(slot, carry):
        tile(slot, y, 0, 1, True)
        return carry

    lax.fori_loop(0, 2, diagonal, 0)

    def step(i, carry):
        arrive(i)
        forward(i)

        def one_slot(slot, c):
            full, end = last_block(PLAIN, slot, 0), last_block(REACH, slot, 0)
            here = (i <= by_class(UP, core, slot)) & (i <= end)

            @pl.when(here & (i <= full))
            def _():
                tile(slot, y, i, 1, False)

            @pl.when(here & (i > full))
            def _():
                tile(slot, y, i, 1, True)

            return c

        lax.fori_loop(0, 2, one_slot, 0)

        @pl.when((core == 0) & (z >= 8 - i))
        def _():
            tile(0, y, 8 - i, 1, False)

        return carry

    lax.fori_loop(1, 5, step, 0)
    for slot in range(2):
        write_dq(y, slot)

    def q_landed(col, half, slot):
        return remote(qd.at[0, 0, 0], qd.at[col, half, slot], s_q.at[0, 0, 0], r_q.at[col, half, slot], sibling)

    def st_landed(col, half):
        return remote(st.at[0, 0], st.at[col, half], s_st.at[0, 0], r_st.at[col, half], sibling)

    forwards = []
    for half in range(2):
        st_landed(before, half).wait_recv()
        forwards.append(remote(st.at[before, half], st.at[before, half], s_fst.at[half], r_st.at[before, half], right))
        forwards[-1].start()
        q_landed(before, half, 0).wait_recv()
        forwards.append(
            remote(qd.at[before, half, 0], qd.at[before, half, 0], s_fq.at[half, 0], r_q.at[before, half, 0], right)
        )
        forwards[-1].start()
        q_landed(after, half, 1).wait_recv()
        forwards.append(
            remote(qd.at[after, half, 1], qd.at[after, half, 1], s_fq.at[half, 1], r_q.at[after, half, 1], left)
        )
        forwards[-1].start()

    def dq_copy(dy, slot):
        col = (y + dy) % 4
        return remote(
            dq_part.at[col, slot], dq_in.at[y, slot], s_dq.at[dy, slot], r_dq.at[y, slot], at(z, col, core)
        )

    def one_column(n, carry):
        dy = n + (n // 2) * (1 - 2 * (n % 2))
        col = (y + dy) % 4
        ahead = col - y
        dq_acc[...] = jnp.zeros_like(dq_acc)
        for half in range(2):

            @pl.when(dy != 3)
            def _(half=half):
                st_landed(col, half).wait_recv()

            @pl.when(dy != 3)
            def _(half=half):
                q_landed(col, half, 0).wait_recv()

            @pl.when(dy != 1)
            def _(half=half):
                q_landed(col, half, 1).wait_recv()

        def one_slot(slot, c):
            first = jnp.where(ahead > 0, 0, 1)
            full, end = last_block(PLAIN, slot, ahead), last_block(REACH, slot, ahead)
            large = (core == 0) & (slot == 0) & (z >= 3)
            below_count = jnp.where(large, 1 - first, jnp.maximum(full - first + 1, 0))
            above_count = jnp.where(large & (z < 7), z - 3, 0)

            def plain(m, cc):
                d = jnp.where(m < below_count, first + m, 4 + m - below_count)
                tile(slot, col, d, 1, False)
                return cc

            lax.fori_loop(0, below_count + above_count, plain, 0)

            def masked(d, cc):
                tile(slot, col, d, 1, True)
                return cc

            lax.fori_loop(jnp.maximum(full + 1, first), end + 1, masked, 0)

            @pl.when(large)
            def _():
                tile(0, col, 1, 3, False)

            @pl.when(large & (z == 7))
            def _():
                tile(0, col, 4, 4, False)

            write_dq(col, slot)
            dq_copy(dy, slot).start()
            return c

        lax.fori_loop(0, 2, one_slot, 0)
        return carry

    lax.fori_loop(1, COLUMNS, one_column, 0)

    def dkv_down(d, slot):
        return remote(
            dkv_send.at[slot, d], dkv_in.at[slot, d - 1], s_ddown.at[slot, d], r_dkv.at[slot, d - 1], below
        )

    def dkv_up(e):
        return remote(dkv_send.at[0, 8 - e], dkv_in.at[0, 9 - e], s_dup.at[e], r_dkv.at[0, 9 - e], above)

    def dkv_landed(slot, d):
        return remote(dkv_send.at[0, 0], dkv_in.at[slot, d], s_dup.at[0], r_dkv.at[slot, d], sibling)

    scales = (SCALING, 1.0)

    def returns_down(i, slot):
        return (z >= i) & (i <= by_class(UP, core, slot))

    def returns_up(i):
        return (core == 0) & ((z + i) % 8 < DOWN)

    def back(n, carry):
        i = 4 - n
        for slot in range(2):
            joined = (z + 1 < PLANES) & (i < by_class(UP, core, slot))

            @pl.when(returns_down(i, slot) & joined)
            def _(slot=slot):
                dkv_landed(slot, i).wait_recv()
                for part in range(2):
                    total = dkv_acc[slot, part, i] * scales[part] + dkv_in[slot, i, part].astype(F32)
                    dkv_send[slot, i, part] = total.astype(BF16)

            @pl.when(returns_down(i, slot) & jnp.logical_not(joined))
            def _(slot=slot):
                for part in range(2):
                    dkv_send[slot, i, part] = (dkv_acc[slot, part, i] * scales[part]).astype(BF16)

            @pl.when(returns_down(i, slot))
            def _(slot=slot):
                dkv_down(i, slot).start()

        @pl.when(returns_up(i) & (i < DOWN))
        def _():
            dkv_landed(0, 8 - i).wait_recv()
            for part in range(2):
                total = dkv_acc[0, part, 8 - i] * scales[part] + dkv_in[0, 8 - i, part].astype(F32)
                dkv_send[0, 8 - i, part] = total.astype(BF16)

        @pl.when(returns_up(i) & (i == DOWN))
        def _():
            for part in range(2):
                dkv_send[0, 4, part] = (dkv_acc[0, part, 4] * scales[part]).astype(BF16)

        @pl.when(returns_up(i))
        def _():
            dkv_up(i).start()

        return carry

    lax.fori_loop(0, 4, back, 0)

    for slot in range(2):
        for dy in range(1, COLUMNS):
            col = (y + dy) % 4
            remote(dq_part.at[0, 0], dq_in.at[col, slot], s_dq.at[0, 0], r_dq.at[col, slot], sibling).wait_recv()
        for part_half in range(2):
            half = core if part_half == 1 else other
            for g in range(GROUP):
                total = dq_part[y, slot, half, g].astype(F32)
                for dy in range(1, COLUMNS):
                    total += dq_in[(y + dy) % 4, slot, half, g].astype(F32)
                fq[part_half, slot, g] = total.astype(BF16)
    q_fin = remote(fq.at[0], fq.at[2], s_fin.at[0], r_fin.at[0], sibling)
    q_fin.start()

    @pl.when(z + 1 < PLANES)
    def _():
        for slot in range(2):
            dkv_landed(slot, 0).wait_recv()
            for part in range(2):
                dkv_acc[slot, part, 0] = dkv_acc[slot, part, 0] * scales[part] + dkv_in[slot, 0, part].astype(F32)

    @pl.when(z + 1 == PLANES)
    def _():
        for slot in range(2):
            dkv_acc[slot, 0, 0] = dkv_acc[slot, 0, 0] * SCALING

    @pl.when((core == 0) & (z < DOWN))
    def _():
        dkv_landed(0, 8).wait_recv()
        for part in range(2):
            dkv_acc[0, part, 0] = dkv_acc[0, part, 0] + dkv_in[0, 8, part].astype(F32)

    for slot in range(2):
        for part in range(2):
            for part_half in range(2):
                half = core if part_half == 1 else other
                rows = pl.ds(pl.multiple_of(half * ROWS, ROWS), ROWS)
                fkv[part_half, slot, part] = dkv_acc[slot, part, 0, rows].astype(BF16)
    kv_fin = remote(fkv.at[0], fkv.at[2], s_fin.at[1], r_fin.at[1], sibling)
    kv_fin.start()
    q_fin.wait_recv()
    kv_fin.wait_recv()

    def entry(kind):
        return 1 + (core + kind // 2) % 2

    for head in range(KV_HEADS):
        masks = [jnp.full((ROWS, HEAD_DIM), chosen_of[kind][head], jnp.int32) > 0 for kind in range(4)]

        def picked(read):
            total = jnp.zeros((ROWS, HEAD_DIM), F32)
            for kind in range(4):
                total = jnp.where(masks[kind], read(entry(kind), kind % 2).astype(F32), total)
            return total.astype(BF16)

        for g in range(GROUP):
            cols = slice((head * GROUP + g) * HEAD_DIM, (head * GROUP + g + 1) * HEAD_DIM)
            dq_out[:, cols] = picked(lambda e, slot, g=g: fq[e, slot, g])
        cols = slice(head * HEAD_DIM, (head + 1) * HEAD_DIM)
        dk_out[:, cols] = picked(lambda e, slot: fkv[e, slot, 0])
        dv_out[:, cols] = picked(lambda e, slot: fkv[e, slot, 1])

    for c in sib_copies + forwards + [q_fin, kv_fin]:
        c.wait_send()
    for half in range(2):
        for way in range(2):
            st_copy(half, way).wait_send()
            for slot in range(2):
                q_copy(half, slot, way).wait_send()
    for dy in range(1, COLUMNS):
        for slot in range(2):
            dq_copy(dy, slot).wait_send()

    def sent(i, carry):
        for slot in range(2):

            @pl.when(goes_up(i, slot))
            def _(slot=slot):
                up_copy(i, slot).wait_send()

            @pl.when((i > 0) & returns_down(i, slot))
            def _(slot=slot):
                dkv_down(i, slot).wait_send()

        @pl.when(goes_down(i))
        def _():
            down_copy(i).wait_send()

        @pl.when((i > 0) & returns_up(i))
        def _():
            dkv_up(i).wait_send()

        return carry

    lax.fori_loop(0, 5, sent, 0)


def per_device(queries, keys, values, outputs, out_grad, log_sum_exp, spans):
    whole = pl.BlockSpec(memory_space=pltpu.VMEM)
    dma = pltpu.SemaphoreType.DMA
    return tuple(
        pl.pallas_call(
            kernel,
            in_specs=[pl.BlockSpec(memory_space=pltpu.SMEM)] + [whole] * 6,
            out_specs=[whole] * 3,
            out_shape=[
                jax.ShapeDtypeStruct((ROWS, Q_HEADS * HEAD_DIM), BF16),
                jax.ShapeDtypeStruct((ROWS, KV_HEADS * HEAD_DIM), BF16),
                jax.ShapeDtypeStruct((ROWS, KV_HEADS * HEAD_DIM), BF16),
            ],
            scratch_shapes=[
                pltpu.VMEM((COLUMNS, 2, 2, 2, GROUP, ROWS, HEAD_DIM), BF16),
                pltpu.VMEM((PLANES, 2, 2, 2, ROWS, HEAD_DIM), BF16),
                pltpu.VMEM((COLUMNS, 2, 2, 8, 256), F32),
                pltpu.VMEM((2, 2, GROUP, ROWS, HEAD_DIM), BF16),
                pltpu.VMEM((2, 2, ROWS, HEAD_DIM), BF16),
                pltpu.VMEM((2, 8, 256), F32),
                pltpu.VMEM((2, 2, 2, HEAD_DIM, 256), F32),
                pltpu.VMEM((2, 2, PLANES, 256, HEAD_DIM), F32),
                pltpu.VMEM((COLUMNS, 2, 2, GROUP, ROWS, HEAD_DIM), BF16),
                pltpu.VMEM((COLUMNS, 2, 2, GROUP, ROWS, HEAD_DIM), BF16),
                pltpu.VMEM((2, PLANES, 2, 256, HEAD_DIM), BF16),
                pltpu.VMEM((2, PLANES + 1, 2, 256, HEAD_DIM), BF16),
                pltpu.VMEM((3, 2, GROUP, ROWS, HEAD_DIM), BF16),
                pltpu.VMEM((3, 2, 2, ROWS, HEAD_DIM), BF16),
                dma((3,)),
                dma((3,)),
                dma((2, 2, 2)),
                dma((2, 2)),
                dma((COLUMNS, 2, 2)),
                dma((COLUMNS, 2)),
                dma((2, 2)),
                dma((2,)),
                dma((PLANES, 2)),
                dma((PLANES,)),
                dma((PLANES, 2)),
                dma((COLUMNS, 2)),
                dma((COLUMNS, 2)),
                dma((PLANES,)),
                dma((2, PLANES)),
                dma((2, PLANES + 1)),
                dma((2,)),
                dma((2,)),
            ],
            compiler_params=pltpu.CompilerParams(
                collective_id=0, has_side_effects=True, vmem_limit_bytes=56 * 2**20
            ),
            name="gradients",
        )(spans, queries, keys, values, outputs, out_grad, log_sum_exp)
    )


def solution(mesh):
    in_specs = (
        P(("dp", "ctx"), None),
        P(("dp", "ctx"), None),
        P(("dp", "ctx"), None),
        P(("dp", "ctx"), None),
        P(("dp", "ctx"), None),
        P(None, ("dp", "ctx")),
        P("dp"),
    )
    out_specs = (P(("dp", "ctx"), None), P(("dp", "ctx"), None), P(("dp", "ctx"), None))
    return jax.shard_map(
        per_device, mesh=mesh, in_specs=in_specs, out_specs=out_specs, check_vma=False
    )
```

time: 1240 us -> 81.4 us (0.07)
  the two profiles are of different devices: /device:TPU:103 before, /device:TPU:1 now
where the time goes in v2:
time: 81.4 us; the launch traced here: 81.2 us
  Pallas kernels  77.1 us (95%)
  local copies, waits for them, and re-layouts  3.53 us (4%)
    pallas_call x1, Pallas kernels, per_device(): pl.pallas_call(kernel, in_specs=[pl.BlockSpec(memory_space=pltpu.SMEM)] +...  77.1 us
    unnamed x7, local copies, waits for them, and re-layouts  3.53 us

profile of v2, /device:TPU:1, one launch (start us, length us, event | category | flops | bytes accessed | tf_op | source)
XLA Modules:
  0.0 81.2 jit_solution(9927158873338192565)
XLA Ops:
  0.6 77.1 %gradients.1 = (bf16[128,2048]{1,0:T(8,128)(2,1)}, bf16[128,512]{1,0:T(8,128)(2,1)}, bf16[128,512]{1,0:T(8,128)(2,1)}) custom-call(s32[4]{0:T(128)} %spans_ref.1, bf16[128,2048]{1,0:T(8,128)(2,1)} %q_ref.1, bf16[128,512]{1,0:T(8,128)(2,1)} %k_ref.1, bf16[128,512]{1,0:T(8,128)(2,1)} %v_ref.1, bf16[128,2048]{1,0:T(8,128)(2,1)} %o_ref.1, ...), custom_call_target="tpu_custom_call" | custom-call | tf_op jit(solution)/shard_map/gradients/pallas_call | solution.py:553
  77.7 0.0 copy-start.1
  77.7 1.9 %copy.13 = bf16[128,2048]{1,0:T(8,128)(2,1)} copy(bf16[128,2048]{1,0:T(8,128)(2,1)} %get-tuple-element.6) | data formatting | bytes 1048576
  79.6 0.0 copy-done.1
  79.6 0.0 copy-start
  79.6 0.7 copy.14
  80.3 0.3 copy-done
  80.6 0.7 copy.15
Async XLA Ops:
  77.7 1.9 %copy-start.1 = (bf16[128,512]{1,0:T(8,128)(2,1)S(1)}, bf16[128,512]{1,0:T(8,128)(2,1)}, u32[]{:S(2)}) copy-start(bf16[128,512]{1,0:T(8,128)(2,1)} %get-tuple-element.7) | copy-start | bytes 393220
  79.6 1.0 %copy-start = (bf16[128,512]{1,0:T(8,128)(2,1)S(1)}, bf16[128,512]{1,0:T(8,128)(2,1)}, u32[]{:S(2)}) copy-start(bf16[128,512]{1,0:T(8,128)(2,1)} %get-tuple-element.8) | copy-start | bytes 393220

commit v3 on v2

v3 whole, which is shorter than its diff:
```python
import functools
import math

import jax
import jax.numpy as jnp
from jax import lax
from jax.experimental import pallas as pl
from jax.experimental.pallas import tpu as pltpu
from jax.sharding import PartitionSpec as P

Q_HEADS = 16
KV_HEADS = 4
GROUP = 4
HEAD_DIM = 128
PLANES = 8
COLUMNS = 4
ROWS = 128
SCALING = 1.0 / math.sqrt(HEAD_DIM)
LOG2E = math.log2(math.e)
BF16 = jnp.bfloat16
F32 = jnp.float32
MESH = pl.DeviceIdType.MESH
NT = (((1,), (1,)), ((), ()))
NN = (((1,), (0,)), ((), ()))
CHIPS = PLANES * COLUMNS
REACH = ((31, 2), (16, 8))
PLAIN = ((31, 0), (7, 3))
UP = (3, 4)
DOWN = 4
NEAR = 2


def dot(a, b, dims=NN):
    return lax.dot_general(a, b, dims, preferred_element_type=F32)


def place():
    me = lax.axis_index("ctx")
    return me // 8, (me // 2) % 4, me % 2


def at(z, y, core):
    return {"ctx": z * 8 + y * 2 + core}


def remote(src, dst, send, recv, device):
    return pltpu.make_async_remote_copy(
        src_ref=src, dst_ref=dst, send_sem=send, recv_sem=recv, device_id=device, device_id_type=MESH
    )


def by_class(table, core, slot):
    first, second = table
    low = first[0] + (first[1] - first[0]) * slot
    high = second[0] + (second[1] - second[0]) * slot
    return low + (high - low) * core


def kernel(
    spans_ref,
    q_ref,
    k_ref,
    v_ref,
    o_ref,
    g_ref,
    lse_ref,
    dq_out,
    dk_out,
    dv_out,
    qd,
    kv,
    kv1,
    st,
    q_sib,
    kv_sib,
    st_sib,
    dq_acc,
    dkv_acc,
    dkv1_acc,
    dq_part,
    dq_in,
    dkv_send,
    dkv_in,
    near_send,
    near_in,
    fq,
    fkv,
    s_sib,
    r_sib,
    s_q,
    s_st,
    r_q,
    r_st,
    s_fq,
    s_fst,
    s_up,
    s_down,
    r_kv,
    s_near,
    r_near,
    s_dq,
    r_dq,
    s_dkv,
    r_dkv,
    s_nback,
    r_nback,
    s_fin,
    r_fin,
):
    z, y, core = place()
    other = 1 - core
    up_reach = UP[0] + (UP[1] - UP[0]) * core
    chip = z * COLUMNS + y
    home = y * core
    sibling = at(z, y, other)
    before, after, across = (y + 3) % 4, (y + 1) % 4, (y + 2) % 4
    left, right, far = at(z, before, core), at(z, after, core), at(z, across, core)
    above, below = at((z + 1) % 8, y, core), at((z + 7) % 8, y, core)

    def at_chip(number):
        return at(number // COLUMNS, number % COLUMNS, core)

    def feeds(j):
        return (core == 0) & (chip + j < CHIPS)

    def fed_by(j):
        return (core == 0) & (chip >= j)

    barrier = pltpu.get_barrier_semaphore()
    for peer in (sibling, left, right, far):
        pl.semaphore_signal(barrier, inc=1, device_id=peer, device_id_type=MESH)
    for dz in range(1, PLANES):
        pl.semaphore_signal(barrier, inc=1, device_id=at((z + dz) % 8, y, core), device_id_type=MESH)
    for j in range(1, NEAR + 1):

        @pl.when(feeds(j))
        def _(j=j):
            pl.semaphore_signal(barrier, inc=1, device_id=at_chip(chip + j), device_id_type=MESH)

        @pl.when(fed_by(j))
        def _(j=j):
            pl.semaphore_signal(barrier, inc=1, device_id=at_chip(chip - j), device_id_type=MESH)

    greetings = 11 + (1 - core) * (jnp.minimum(NEAR, chip) + jnp.minimum(NEAR, CHIPS - 1 - chip))

    spans = [spans_ref[i] for i in range(KV_HEADS)]
    tops = ((4096, 8192), (0, 512), (2048, 4096), (1024, 2048))
    chosen_of, limits = [], []
    for low, top in tops:
        picks = [jnp.where((span > low) & (span <= top), 1, 0) for span in spans]
        chosen_of.append(picks)
        limits.append(sum(pick * span for pick, span in zip(picks, spans)))

    def taker(picks):
        weights = [pick.astype(F32) for pick in picks]

        def taken(ref, g, width):
            total = None
            for head in range(KV_HEADS):
                first = head * width + g * HEAD_DIM
                term = ref[:, first : first + HEAD_DIM] * weights[head].astype(BF16)
                total = term if total is None else total + term
            return total

        return weights, taken

    def pack_queries(picks, q_to, st_to):
        weights, taken = taker(picks)
        st_to[...] = jnp.zeros((8, 256), F32)
        for g in range(GROUP):
            grad = taken(g_ref, g, 512)
            q_to[0, g] = taken(q_ref, g, 512)
            q_to[1, g] = grad
            product = grad.astype(F32) * taken(o_ref, g, 512).astype(F32)
            lanes = slice((g % 2) * ROWS, (g % 2 + 1) * ROWS)
            lse = sum(
                lse_ref[head * GROUP + g : head * GROUP + g + 1, :] * weights[head] for head in range(KV_HEADS)
            )
            st_to[g // 2 : g // 2 + 1, lanes] = lse * LOG2E
            st_to[2 + g // 2 : 3 + g // 2, lanes] = jnp.sum(product.T, axis=0, keepdims=True)

    def pack_keys(picks, kv_to):
        taken = taker(picks)[1]
        kv_to[0] = taken(k_ref, 0, HEAD_DIM)
        kv_to[1] = taken(v_ref, 0, HEAD_DIM)

    theirs = [
        [jnp.where(core == 0, a, b) for a, b in zip(chosen_of[2 + slot], chosen_of[slot])] for slot in range(2)
    ]
    ours = [[jnp.where(core == 0, a, b) for a, b in zip(chosen_of[slot], chosen_of[2 + slot])] for slot in range(2)]

    def q_copy(half, slot, way):
        return remote(
            qd.at[y, half, slot],
            qd.at[y, half, slot],
            s_q.at[half, slot, way],
            r_q.at[y, half, slot],
            right if way == 0 else left,
        )

    def st_copy(half, slot, way):
        return remote(
            st.at[y, half, slot],
            st.at[y, half, slot],
            s_st.at[half, slot, way],
            r_st.at[y, half, slot],
            right if way == 0 else left,
        )

    def start_q(half, slot):
        for way in range(2):
            st_copy(half, slot, way).start()
            q_copy(half, slot, way).start()

    sib_copies = [
        remote(kv_sib.at[0], kv.at[0, core], s_sib.at[4], r_sib.at[4], sibling),
    ]
    for slot in range(2):
        sib_copies.append(remote(q_sib.at[slot], qd.at[y, core, slot], s_sib.at[slot], r_sib.at[slot], sibling))
        sib_copies.append(
            remote(st_sib.at[slot], st.at[y, core, slot], s_sib.at[2 + slot], r_sib.at[2 + slot], sibling)
        )

    sib_copies.append(remote(kv_sib.at[1], kv1.at[y * other, core], s_sib.at[5], r_sib.at[5], sibling))

    for slot in range(2):
        pack_keys(theirs[slot], kv_sib.at[slot])
    pl.semaphore_wait(barrier, greetings)
    sib_copies[0].start()
    sib_copies[5].start()
    pack_keys(ours[0], kv.at[0, core])
    pack_keys(ours[1], kv1.at[home, core])
    pack_queries(theirs[0], q_sib.at[0], st_sib.at[0])
    sib_copies[1].start()
    sib_copies[2].start()
    pack_queries(ours[0], qd.at[y, core, 0], st.at[y, core, 0])
    start_q(core, 0)

    def up_copy(d, part):
        return remote(
            kv.at[d, :, part], kv.at[d + 1, :, part], s_up.at[d, part], r_kv.at[d + 1, part], above
        )

    def down_copy(e, part):
        return remote(
            kv.at[(8 - e) % 8, :, part], kv.at[7 - e, :, part], s_down.at[e, part], r_kv.at[7 - e, part], below
        )

    def goes_up(d):
        return (z + 1 < PLANES) & (z >= d) & (d < up_reach)

    def goes_down(e):
        return (core == 0) & (e < DOWN) & ((z + e) % 8 < DOWN)

    def kv_landed(d, part):
        return remote(kv.at[0, :, 0], kv.at[d, :, part], s_up.at[0, 0], r_kv.at[d, part], sibling)

    def hop(i):
        for part in range(2):
            if not isinstance(i, int):

                @pl.when((z >= i) & (i <= up_reach))
                def _(part=part):
                    kv_landed(i, part).wait_recv()

            @pl.when(goes_up(i))
            def _(part=part):
                up_copy(i, part).start()

            if not isinstance(i, int):

                @pl.when((core == 0) & ((z + i) % 8 < DOWN))
                def _(part=part):
                    kv_landed(8 - i, part).wait_recv()

            @pl.when(goes_down(i))
            def _(part=part):
                down_copy(i, part).start()

    def near_copy(j):
        return remote(kv1.at[0], kv1.at[j], s_near.at[j], r_near.at[j], at_chip(chip + j))

    def lift_copy(d):
        return remote(kv1.at[4 * d + y], kv1.at[4 * d + 4 + y], s_near.at[d], r_near.at[4 * d + 4 + y], above)

    def round_copy(d, dy):
        block = 4 * d + y
        return remote(kv1.at[block], kv1.at[block], s_near.at[3 * d + dy + 2], r_near.at[block], at(z, (y + dy) % 4, core))

    def near_landed(block):
        return remote(kv1.at[0], kv1.at[block], s_near.at[0], r_near.at[block], sibling)

    def lifts(d):
        return (core == 1) & (d < 2) & (z >= d) & (z + 1 < PLANES)

    def rounds(d, dy):
        col = (y + dy) % 4
        blocks = 4 * d + col - y
        return (core == 1) & (z >= d) & (blocks >= 0) & (blocks <= REACH[1][1])

    def lift(d):
        if d > 0:

            @pl.when((core == 1) & (z >= d))
            def _():
                near_landed(4 * d + y).wait_recv()

        if d < 2:

            @pl.when(lifts(d))
            def _():
                lift_copy(d).start()

        for dy in (1, 3, 2):

            @pl.when(rounds(d, dy))
            def _(dy=dy):
                round_copy(d, dy).start()

    def start_near():
        for j in range(1, NEAR + 1):

            @pl.when(feeds(j))
            def _(j=j):
                near_copy(j).start()

        lift(0)

    sib_copies[0].wait_recv()
    hop(0)
    sib_copies[5].wait_recv()
    start_near()
    pack_queries(theirs[1], q_sib.at[1], st_sib.at[1])
    sib_copies[3].start()
    sib_copies[4].start()
    sib_copies[1].wait_recv()
    sib_copies[2].wait_recv()
    start_q(other, 0)
    pack_queries(ours[1], qd.at[y, core, 1], st.at[y, core, 1])

    dkv_acc[...] = jnp.zeros_like(dkv_acc)
    dkv1_acc[...] = jnp.zeros_like(dkv1_acc)
    own_limits = [jnp.where(core == 0, limits[slot], limits[2 + slot]) for slot in range(2)]

    def tile(slot, col, d0, count, masked, blocks=0):
        size = count * 256
        keys, acc = (kv, dkv_acc) if slot == 0 else (kv1, dkv1_acc)
        into = pl.ds(d0, count)
        k = keys[pl.ds(d0, count), :, 0].reshape(size, HEAD_DIM)
        v = keys[pl.ds(d0, count), :, 1].reshape(size, HEAD_DIM)
        k_t = k.T
        base = d0 * 1024 + (col - y) * 256 if slot == 0 else blocks * 256
        if count == 1:
            groups = [[(half, pair) for half in range(2) for pair in range(2)]]
        else:
            groups = [[(half, pair)] for half in range(2) for pair in range(2)]
        for group in groups:
            width = 256 * len(group)

            def rows(what, group=group, width=width):
                return jnp.concatenate(
                    [
                        qd[col, half, slot, what, 2 * pair : 2 * pair + 2].reshape(256, HEAD_DIM)
                        for half, pair in group
                    ],
                    axis=0,
                )

            def stats(first, group=group):
                return jnp.concatenate(
                    [st[col, half, slot, first + pair : first + pair + 1] for half, pair in group], axis=1
                )

            q, g = rows(0), rows(1)
            prob = jnp.exp2(dot(k, q, NT) * (SCALING * LOG2E) - stats(0))
            if masked:
                key = lax.broadcasted_iota(jnp.int32, (size, width), 0)
                lane = lax.broadcasted_iota(jnp.int32, (size, width), 1)
                row = lane % ROWS + lane // 512 * ROWS
                distance = row - key + base
                prob = jnp.where((distance >= 0) & (distance < own_limits[slot]), prob, 0.0)
            ds = (prob * (dot(v, g, NT) - stats(2))).astype(BF16)
            low = prob.astype(BF16)
            acc[0, into] += dot(ds, q).reshape(count, 256, HEAD_DIM)
            acc[1, into] += dot(low, g).reshape(count, 256, HEAD_DIM)
            change = dot(k_t, ds)
            for n, (half, pair) in enumerate(group):
                dq_acc[slot, half, pair] += change[:, n * 256 : (n + 1) * 256]

    def last_block(table, slot, ahead):
        return jnp.minimum(z, (by_class(table, core, slot) - ahead + 4) // 4 - 1)

    def write_dq(col, slot):
        for half in range(2):
            for pair in range(2):
                total = dq_acc[slot, half, pair].T * SCALING
                dq_part[col, slot, half, 2 * pair : 2 * pair + 2] = total.reshape(2, ROWS, HEAD_DIM).astype(BF16)

    def q_landed(col, half, slot):
        return remote(qd.at[0, 0, 0], qd.at[col, half, slot], s_q.at[0, 0, 0], r_q.at[col, half, slot], sibling)

    def st_landed(col, half, slot):
        return remote(st.at[0, 0, 0], st.at[col, half, slot], s_st.at[0, 0, 0], r_st.at[col, half, slot], sibling)

    def q_forward(slot, half):
        col, to = (before, right) if half == 0 else (after, left)
        return (
            remote(
                st.at[col, half, slot], st.at[col, half, slot], s_fst.at[slot, half], r_st.at[col, half, slot], to
            ),
            remote(qd.at[col, half, slot], qd.at[col, half, slot], s_fq.at[slot, half], r_q.at[col, half, slot], to),
        )

    def pass_queries(slot):
        for half in range(2):
            col = before if half == 0 else after
            st_landed(col, half, slot).wait_recv()
            q_landed(col, half, slot).wait_recv()
            for c in q_forward(slot, half):
                c.start()

    def await_queries(slot, dy):
        col = (y + dy) % 4
        for half in range(2):

            @pl.when((dy != 3) if half == 0 else (dy != 1))
            def _(half=half):
                st_landed(col, half, slot).wait_recv()
                q_landed(col, half, slot).wait_recv()

    dq_acc[...] = jnp.zeros_like(dq_acc)
    tile(0, y, 0, 1, True)

    def step(i, carry):
        @pl.when(i == 4)
        def _():
            pass_queries(0)

        hop(i)

        @pl.when(i == 3)
        def _():
            lift(1)

        @pl.when(i == 4)
        def _():
            lift(2)

        full, end = last_block(PLAIN, 0, 0), last_block(REACH, 0, 0)
        here = (i <= up_reach) & (i <= end)

        @pl.when(here & (i <= full))
        def _():
            tile(0, y, i, 1, False)

        @pl.when(here & (i > full))
        def _():
            tile(0, y, i, 1, True)

        @pl.when((core == 0) & (z >= 8 - i))
        def _():
            tile(0, y, 8 - i, 1, False)

        return carry

    lax.fori_loop(1, 5, step, 0)
    write_dq(y, 0)
    sib_copies[3].wait_recv()
    sib_copies[4].wait_recv()

    def dq_copy(dy):
        col = (y + dy) % 4
        return remote(dq_part.at[col, 0], dq_in.at[y], s_dq.at[dy], r_dq.at[y], at(z, col, core))

    scales = (SCALING, 1.0)

    def dkv_landed(d):
        return remote(dkv_send.at[0], dkv_in.at[d], s_dkv.at[0], r_dkv.at[d], sibling)

    def dkv_back(d):
        return remote(dkv_send.at[d], dkv_in.at[d], s_dkv.at[d], r_dkv.at[d], at((z + 8 - d) % 8, y, core))

    def dkv_join(d):
        return remote(dkv_send.at[d], dkv_in.at[d], s_dkv.at[d], r_dkv.at[d], at((z + 10 - d) % 8, y, core))

    def ready(d):
        for part in range(2):
            dkv_send[d, part] = (dkv_acc[part, d] * scales[part]).astype(BF16)

    def start_back(d):
        ready(d)
        dkv_back(d).start()

    def first_level():
        @pl.when((core == 1) & (z >= 4))
        def _():
            ready(4)
            dkv_join(4).start()

        @pl.when(z >= 3)
        def _():
            ready(3)
            dkv_join(3).start()

        @pl.when(z >= 1)
        def _():
            start_back(1)

    def second_level():
        @pl.when(z >= 2)
        def _():
            for part in range(2):
                dkv_acc[part, 2] = dkv_acc[part, 2] * scales[part]

            for d in (3, 4):

                @pl.when((z + d - 2 < PLANES) & (core >= d - 3))
                def _(d=d):
                    dkv_landed(d).wait_recv()
                    for part in range(2):
                        dkv_acc[part, 2] = dkv_acc[part, 2] + dkv_in[d, part].astype(F32)

            for part in range(2):
                dkv_send[2, part] = dkv_acc[part, 2].astype(BF16)
            dkv_back(2).start()

    def near_back(j):
        return remote(near_send.at[j], near_in.at[j], s_nback.at[j], r_nback.at[j], at_chip(chip - j))

    def lower_back(d):
        block = 4 * d + y
        return remote(
            near_send.at[block], near_in.at[block], s_nback.at[block], r_nback.at[block], at((z + 8 - d) % 8, y, core)
        )

    def round_back(block):
        entry = block - block % 4 + y
        return remote(
            near_send.at[block], near_in.at[entry], s_nback.at[block], r_nback.at[entry], at(z, block % 4, core)
        )

    def near_back_landed(block):
        return remote(near_send.at[0], near_in.at[block], s_nback.at[0], r_nback.at[block], sibling)

    def place_of(t):
        d, col = 2 - t // 4, t % 4
        block = (1 - core) * t + core * (4 * d + col)
        blocks = (1 - core) * t + core * (4 * d + y - col)
        return d, col, block, blocks

    def middle_sees(d, seer, col):
        blocks = 4 * d + seer - col
        return (core == 1) & (z >= d) & (blocks >= 0) & (blocks <= REACH[1][1])

    def second(t, carry):
        d, col, block, blocks = place_of(t)
        short = (core == 0) & (chip >= blocks)
        middle = (core == 1) & (z >= d) & (blocks >= 0) & (blocks <= REACH[1][1])

        @pl.when(short | middle)
        def _():
            @pl.when(((core == 0) & (blocks > 0)) | ((core == 1) & (col != y)))
            def _():
                near_landed(block).wait_recv()

            plain = (core == 1) & (blocks >= 1) & (blocks <= PLAIN[1][1])

            @pl.when(plain)
            def _():
                tile(1, y, block, 1, False, blocks)

            @pl.when(jnp.logical_not(plain))
            def _():
                tile(1, y, block, 1, True, blocks)

            for part in range(2):
                near_send[block, part] = (dkv1_acc[part, block] * scales[part]).astype(BF16)

            @pl.when((core == 0) & (blocks > 0))
            def _():
                near_back(block).start()

            @pl.when((core == 1) & (col != y))
            def _():
                round_back(block).start()

        return carry

    def join(d):
        @pl.when(core == 1)
        def _():
            for part in range(2):
                dkv1_acc[part, 4 * d + y] = dkv1_acc[part, 4 * d + y] * scales[part]

        for dy in range(1, COLUMNS):
            col = (y + dy) % 4

            @pl.when(middle_sees(d, col, y))
            def _(col=col):
                near_back_landed(4 * d + col).wait_recv()
                for part in range(2):
                    dkv1_acc[part, 4 * d + y] = dkv1_acc[part, 4 * d + y] + near_in[4 * d + col, part].astype(F32)

        if d > 0:

            @pl.when((core == 1) & (z >= d))
            def _():
                for part in range(2):
                    near_send[4 * d + y, part] = dkv1_acc[part, 4 * d + y].astype(BF16)
                lower_back(d).start()

    def nth(n):
        return n + (n // 2) * (1 - 2 * (n % 2))

    def one_column(n):
        dy = nth(n)
        col = (y + dy) % 4
        ahead = col - y
        await_queries(0, dy)
        dq_acc[0] = jnp.zeros_like(dq_acc[0])
        first = jnp.where(ahead > 0, 0, 1)
        full, end = last_block(PLAIN, 0, ahead), last_block(REACH, 0, ahead)
        large = (core == 0) & (z >= 3)
        below_count = jnp.where(large, 1 - first, jnp.maximum(full - first + 1, 0))
        above_count = jnp.where(large & (z < 7), z - 3, 0)

        @pl.when(large & (z == 7))
        def _():
            tile(0, col, 4, 4, False)

            @pl.when(n == 3)
            def _():
                for d in range(4, PLANES):
                    start_back(d)

        def plain(m, cc):
            d = jnp.where(m < below_count, first + m, 4 + m - below_count)
            tile(0, col, d, 1, False)
            return cc

        lax.fori_loop(0, below_count + above_count, plain, 0)

        def masked(d, cc):
            tile(0, col, d, 1, True)
            return cc

        lax.fori_loop(jnp.maximum(full + 1, first), end + 1, masked, 0)

        @pl.when(large)
        def _():
            tile(0, col, 1, 3, False)

        write_dq(col, 0)
        dq_copy(dy).start()


    def phase(n, carry):
        one_column(n)

        @pl.when(n == 3)
        def _():
            first_level()

            def rest_back(d, cc):
                start_back(d)
                return cc

            lax.fori_loop(4, jnp.where((core == 0) & (z < 7), z + 1, 4), rest_back, 0)

        return carry

    lax.fori_loop(1, COLUMNS, phase, 0)

    def slot_one(t, carry):
        @pl.when(t == 8)
        def _():
            second_level()
            join(2)

        second(t, 0)
        return carry

    lax.fori_loop(0, jnp.where(core == 1, 12, NEAR + 1), slot_one, 0)
    write_dq(y, 1)
    join(1)

    @pl.when(core == 0)
    def _():
        second_level()

    join(0)

    for dy in range(1, COLUMNS):
        col = (y + dy) % 4
        remote(dq_part.at[0, 0], dq_in.at[col], s_dq.at[0], r_dq.at[col], sibling).wait_recv()
    for part_half in range(2):
        half = core if part_half == 1 else other
        for g in range(GROUP):
            total = dq_part[y, 0, half, g].astype(F32)
            for dy in range(1, COLUMNS):
                total += dq_in[(y + dy) % 4, half, g].astype(F32)
            fq[part_half, 0, g] = total.astype(BF16)
            fq[part_half, 1, g] = dq_part[y, 1, half, g]
    q_fin = remote(fq.at[0], fq.at[2], s_fin.at[0], r_fin.at[0], sibling)
    q_fin.start()

    def add_near(block):
        near_back_landed(block).wait_recv()
        for part in range(2):
            dkv1_acc[part, home] = dkv1_acc[part, home] + near_in[block, part].astype(F32)

    @pl.when(core == 0)
    def _():
        dkv1_acc[0, 0] = dkv1_acc[0, 0] * SCALING

    for j in range(1, NEAR + 1):

        @pl.when(feeds(j))
        def _(j=j):
            add_near(j)

    for d in (1, 2):

        @pl.when((core == 1) & (z + d < PLANES))
        def _(d=d):
            add_near(4 * d + y)

    dkv_acc[0, 0] = dkv_acc[0, 0] * SCALING

    for d in (1, 2, 4, 5, 6, 7):

        @pl.when((z + d < PLANES) & ((core == 0) | (d < 3)))
        def _(d=d):
            dkv_landed(d).wait_recv()
            for part in range(2):
                dkv_acc[part, 0] = dkv_acc[part, 0] + dkv_in[d, part].astype(F32)

    for slot in range(2):
        for part in range(2):
            for part_half in range(2):
                half = core if part_half == 1 else other
                rows = pl.ds(pl.multiple_of(half * ROWS, ROWS), ROWS)
                acc, entry = (dkv_acc, 0) if slot == 0 else (dkv1_acc, home)
                fkv[part_half, slot, part] = acc[part, entry, rows].astype(BF16)
    kv_fin = remote(fkv.at[0], fkv.at[2], s_fin.at[1], r_fin.at[1], sibling)
    kv_fin.start()
    q_fin.wait_recv()
    kv_fin.wait_recv()

    def entry(kind):
        return 1 + (core + kind // 2) % 2

    for head in range(KV_HEADS):
        masks = [jnp.full((ROWS, HEAD_DIM), chosen_of[kind][head], jnp.int32) > 0 for kind in range(4)]

        def picked(read):
            total = jnp.zeros((ROWS, HEAD_DIM), F32)
            for kind in range(4):
                total = jnp.where(masks[kind], read(entry(kind), kind % 2).astype(F32), total)
            return total.astype(BF16)

        for g in range(GROUP):
            cols = slice((head * GROUP + g) * HEAD_DIM, (head * GROUP + g + 1) * HEAD_DIM)
            dq_out[:, cols] = picked(lambda e, slot, g=g: fq[e, slot, g])
        cols = slice(head * HEAD_DIM, (head + 1) * HEAD_DIM)
        dk_out[:, cols] = picked(lambda e, slot: fkv[e, slot, 0])
        dv_out[:, cols] = picked(lambda e, slot: fkv[e, slot, 1])

    for c in sib_copies + [q_fin, kv_fin]:
        c.wait_send()
    for half in range(2):
        for c in q_forward(0, half):
            c.wait_send()
        for way in range(2):
            st_copy(half, 0, way).wait_send()
            q_copy(half, 0, way).wait_send()
    for dy in range(1, COLUMNS):
        dq_copy(dy).wait_send()

    def sent(i, carry):
        for part in range(2):

            @pl.when(goes_up(i))
            def _(part=part):
                up_copy(i, part).wait_send()

            @pl.when(goes_down(i))
            def _(part=part):
                down_copy(i, part).wait_send()

        return carry

    lax.fori_loop(0, 5, sent, 0)

    for d in range(1, PLANES):

        @pl.when((z >= d) & ((core == 0) | (d <= UP[1])))
        def _(d=d):
            dkv_back(d).wait_send()

    for j in range(1, NEAR + 1):

        @pl.when(feeds(j))
        def _(j=j):
            near_copy(j).wait_send()

    for d in range(3):

        @pl.when(lifts(d))
        def _(d=d):
            lift_copy(d).wait_send()

        for dy in range(1, COLUMNS):

            @pl.when(rounds(d, dy))
            def _(d=d, dy=dy):
                round_copy(d, dy).wait_send()

            col = (y + dy) % 4

            @pl.when(middle_sees(d, y, col))
            def _(d=d, col=col):
                round_back(4 * d + col).wait_send()

        if d > 0:

            @pl.when((core == 1) & (z >= d))
            def _(d=d):
                lower_back(d).wait_send()

    for j in range(1, NEAR + 1):

        @pl.when(fed_by(j))
        def _(j=j):
            near_back(j).wait_send()


def per_device(queries, keys, values, outputs, out_grad, log_sum_exp, spans):
    whole = pl.BlockSpec(memory_space=pltpu.VMEM)
    dma = pltpu.SemaphoreType.DMA
    near_count = 3 * COLUMNS
    return tuple(
        pl.pallas_call(
            kernel,
            in_specs=[pl.BlockSpec(memory_space=pltpu.SMEM)] + [whole] * 6,
            out_specs=[whole] * 3,
            out_shape=[
                jax.ShapeDtypeStruct((ROWS, Q_HEADS * HEAD_DIM), BF16),
                jax.ShapeDtypeStruct((ROWS, KV_HEADS * HEAD_DIM), BF16),
                jax.ShapeDtypeStruct((ROWS, KV_HEADS * HEAD_DIM), BF16),
            ],
            scratch_shapes=[
                pltpu.VMEM((COLUMNS, 2, 2, 2, GROUP, ROWS, HEAD_DIM), BF16),
                pltpu.VMEM((PLANES, 2, 2, ROWS, HEAD_DIM), BF16),
                pltpu.VMEM((near_count, 2, 2, ROWS, HEAD_DIM), BF16),
                pltpu.VMEM((COLUMNS, 2, 2, 8, 256), F32),
                pltpu.VMEM((2, 2, GROUP, ROWS, HEAD_DIM), BF16),
                pltpu.VMEM((2, 2, ROWS, HEAD_DIM), BF16),
                pltpu.VMEM((2, 8, 256), F32),
                pltpu.VMEM((2, 2, 2, HEAD_DIM, 256), F32),
                pltpu.VMEM((2, PLANES, 256, HEAD_DIM), F32),
                pltpu.VMEM((2, near_count, 256, HEAD_DIM), F32),
                pltpu.VMEM((COLUMNS, 2, 2, GROUP, ROWS, HEAD_DIM), BF16),
                pltpu.VMEM((COLUMNS, 2, GROUP, ROWS, HEAD_DIM), BF16),
                pltpu.VMEM((PLANES, 2, 256, HEAD_DIM), BF16),
                pltpu.VMEM((PLANES, 2, 256, HEAD_DIM), BF16),
                pltpu.VMEM((near_count, 2, 256, HEAD_DIM), BF16),
                pltpu.VMEM((near_count, 2, 256, HEAD_DIM), BF16),
                pltpu.VMEM((3, 2, GROUP, ROWS, HEAD_DIM), BF16),
                pltpu.VMEM((3, 2, 2, ROWS, HEAD_DIM), BF16),
                dma((6,)),
                dma((6,)),
                dma((2, 2, 2)),
                dma((2, 2, 2)),
                dma((COLUMNS, 2, 2)),
                dma((COLUMNS, 2, 2)),
                dma((2, 2)),
                dma((2, 2)),
                dma((PLANES, 2)),
                dma((PLANES, 2)),
                dma((PLANES, 2)),
                dma((near_count,)),
                dma((near_count,)),
                dma((COLUMNS,)),
                dma((COLUMNS,)),
                dma((PLANES,)),
                dma((PLANES,)),
                dma((near_count,)),
                dma((near_count,)),
                dma((2,)),
                dma((2,)),
            ],
            compiler_params=pltpu.CompilerParams(
                collective_id=0, has_side_effects=True, vmem_limit_bytes=56 * 2**20
            ),
            name="gradients",
        )(spans, queries, keys, values, outputs, out_grad, log_sum_exp)
    )


def solution(mesh):
    in_specs = (
        P(("dp", "ctx"), None),
        P(("dp", "ctx"), None),
        P(("dp", "ctx"), None),
        P(("dp", "ctx"), None),
        P(("dp", "ctx"), None),
        P(None, ("dp", "ctx")),
        P("dp"),
    )
    out_specs = (P(("dp", "ctx"), None), P(("dp", "ctx"), None), P(("dp", "ctx"), None))
    return jax.shard_map(
        per_device, mesh=mesh, in_specs=in_specs, out_specs=out_specs, check_vma=False
    )
```

time: 81.4 us -> 72.1 us (0.89)
  the two profiles are of different devices: /device:TPU:1 before, /device:TPU:103 now
where the time goes in v3:
time: 72.1 us; the launch traced here: 71.9 us
  Pallas kernels  67.7 us (94%)
  local copies, waits for them, and re-layouts  3.53 us (5%)
    pallas_call x1, Pallas kernels, per_device(): pl.pallas_call(kernel, in_specs=[pl.BlockSpec(memory_space=pltpu.SMEM)] +...  67.7 us
    unnamed x7, local copies, waits for them, and re-layouts  3.53 us

profile of v3, /device:TPU:103, one launch (start us, length us, event | category | flops | bytes accessed | tf_op | source)
XLA Modules:
  0.0 71.9 jit_solution(18394623850892379636)
XLA Ops:
  0.6 67.7 %gradients.1 = (bf16[128,2048]{1,0:T(8,128)(2,1)}, bf16[128,512]{1,0:T(8,128)(2,1)}, bf16[128,512]{1,0:T(8,128)(2,1)}) custom-call(s32[4]{0:T(128)} %spans_ref.1, bf16[128,2048]{1,0:T(8,128)(2,1)} %q_ref.1, bf16[128,512]{1,0:T(8,128)(2,1)} %k_ref.1, bf16[128,512]{1,0:T(8,128)(2,1)} %v_ref.1, bf16[128,2048]{1,0:T(8,128)(2,1)} %o_ref.1, ...), custom_call_target="tpu_custom_call" | custom-call | tf_op jit(solution)/shard_map/gradients/pallas_call | solution.py:843
  68.3 0.0 copy-start.1
  68.3 1.9 %copy.13 = bf16[128,2048]{1,0:T(8,128)(2,1)} copy(bf16[128,2048]{1,0:T(8,128)(2,1)} %get-tuple-element.6) | data formatting | bytes 1048576
  70.3 0.0 copy-done.1
  70.3 0.0 copy-start
  70.3 0.7 copy.14
  70.9 0.3 copy-done
  71.2 0.7 copy.15
Async XLA Ops:
  68.3 1.9 %copy-start.1 = (bf16[128,512]{1,0:T(8,128)(2,1)S(1)}, bf16[128,512]{1,0:T(8,128)(2,1)}, u32[]{:S(2)}) copy-start(bf16[128,512]{1,0:T(8,128)(2,1)} %get-tuple-element.7) | copy-start | bytes 393220
  70.3 1.0 %copy-start = (bf16[128,512]{1,0:T(8,128)(2,1)S(1)}, bf16[128,512]{1,0:T(8,128)(2,1)}, u32[]{:S(2)}) copy-start(bf16[128,512]{1,0:T(8,128)(2,1)} %get-tuple-element.8) | copy-start | bytes 393220

commit v4 on v3

--- a/solution.py
+++ b/solution.py
@@ -225,7 +225,9 @@
 
     for slot in range(2):
         pack_keys(theirs[slot], kv_sib.at[slot])
+    pack_queries(ours[0], qd.at[y, core, 0], st.at[y, core, 0])
     pl.semaphore_wait(barrier, greetings)
+    start_q(core, 0)
     sib_copies[0].start()
     sib_copies[5].start()
     pack_keys(ours[0], kv.at[0, core])
@@ -233,8 +235,6 @@
     pack_queries(theirs[0], q_sib.at[0], st_sib.at[0])
     sib_copies[1].start()
     sib_copies[2].start()
-    pack_queries(ours[0], qd.at[y, core, 0], st.at[y, core, 0])
-    start_q(core, 0)
 
     def up_copy(d, part):
         return remote(
@@ -311,12 +311,6 @@
             def _():
                 lift_copy(d).start()
 
-        for dy in (1, 3, 2):
-
-            @pl.when(rounds(d, dy))
-            def _(dy=dy):
-                round_copy(d, dy).start()
-
     def start_near():
         for j in range(1, NEAR + 1):
 
@@ -324,11 +318,18 @@
             def _(j=j):
                 near_copy(j).start()
 
-        lift(0)
+    def start_rounds():
+        for d in range(3):
+            for dy in (1, 3, 2):
+
+                @pl.when(rounds(d, dy))
+                def _(d=d, dy=dy):
+                    round_copy(d, dy).start()
 
     sib_copies[0].wait_recv()
     hop(0)
     sib_copies[5].wait_recv()
+    lift(0)
     start_near()
     pack_queries(theirs[1], q_sib.at[1], st_sib.at[1])
     sib_copies[3].start()
@@ -411,13 +412,16 @@
             remote(qd.at[col, half, slot], qd.at[col, half, slot], s_fq.at[slot, half], r_q.at[col, half, slot], to),
         )
 
-    def pass_queries(slot):
+    def pass_queries(slot, which):
         for half in range(2):
-            col = before if half == 0 else after
-            st_landed(col, half, slot).wait_recv()
-            q_landed(col, half, slot).wait_recv()
-            for c in q_forward(slot, half):
-                c.start()
+
+            @pl.when(which == half)
+            def _(half=half):
+                col = before if half == 0 else after
+                st_landed(col, half, slot).wait_recv()
+                q_landed(col, half, slot).wait_recv()
+                for c in q_forward(slot, half):
+                    c.start()
 
     def await_queries(slot, dy):
         col = (y + dy) % 4
@@ -427,50 +431,6 @@
             def _(half=half):
                 st_landed(col, half, slot).wait_recv()
                 q_landed(col, half, slot).wait_recv()
-
-    dq_acc[...] = jnp.zeros_like(dq_acc)
-    tile(0, y, 0, 1, True)
-
-    def step(i, carry):
-        @pl.when(i == 4)
-        def _():
-            pass_queries(0)
-
-        hop(i)
-
-        @pl.when(i == 3)
-        def _():
-            lift(1)
-
-        @pl.when(i == 4)
-        def _():
-            lift(2)
-
-        full, end = last_block(PLAIN, 0, 0), last_block(REACH, 0, 0)
-        here = (i <= up_reach) & (i <= end)
-
-        @pl.when(here & (i <= full))
-        def _():
-            tile(0, y, i, 1, False)
-
-        @pl.when(here & (i > full))
-        def _():
-            tile(0, y, i, 1, True)
-
-        @pl.when((core == 0) & (z >= 8 - i))
-        def _():
-            tile(0, y, 8 - i, 1, False)
-
-        return carry
-
-    lax.fori_loop(1, 5, step, 0)
-    write_dq(y, 0)
-    sib_copies[3].wait_recv()
-    sib_copies[4].wait_recv()
-
-    def dq_copy(dy):
-        col = (y + dy) % 4
-        return remote(dq_part.at[col, 0], dq_in.at[y], s_dq.at[dy], r_dq.at[y], at(z, col, core))
 
     scales = (SCALING, 1.0)
 
@@ -585,6 +545,65 @@
                 round_back(block).start()
 
         return carry
+
+    dq_acc[...] = jnp.zeros_like(dq_acc)
+    tile(0, y, 0, 1, True)
+
+    def step(i, carry):
+        @pl.when(i == 3)
+        def _():
+            pass_queries(0, core)
+
+        @pl.when(i == 4)
+        def _():
+            pass_queries(0, other)
+
+        hop(i)
+
+        @pl.when(i == 1)
+        def _():
+            sib_copies[3].wait_recv()
+            sib_copies[4].wait_recv()
+
+        @pl.when(i == 2)
+        def _():
+            lift(1)
+
+        @pl.when(i == 3)
+        def _():
+            lift(2)
+
+        @pl.when(i == 4)
+        def _():
+            start_rounds()
+
+        full, end = last_block(PLAIN, 0, 0), last_block(REACH, 0, 0)
+        here = (i <= up_reach) & (i <= end)
+
+        @pl.when(here & (i <= full))
+        def _():
+            tile(0, y, i, 1, False)
+
+        @pl.when(here & (i > full))
+        def _():
+            tile(0, y, i, 1, True)
+
+        @pl.when((core == 0) & (z >= 8 - i))
+        def _():
+            tile(0, y, 8 - i, 1, False)
+
+        @pl.when(i < 4)
+        def _():
+            second((1 - core) * (i - 1) + core * (4 * (3 - i) + y), 0)
+
+        return carry
+
+    lax.fori_loop(1, 5, step, 0)
+    write_dq(y, 0)
+
+    def dq_copy(dy):
+        col = (y + dy) % 4
+        return remote(dq_part.at[col, 0], dq_in.at[y], s_dq.at[dy], r_dq.at[y], at(z, col, core))
 
     def join(d):
         @pl.when(core == 1)
@@ -677,19 +696,30 @@
             second_level()
             join(2)
 
-        second(t, 0)
+        @pl.when(t % 4 != y)
+        def _():
+            second(t, 0)
+
         return carry
 
-    lax.fori_loop(0, jnp.where(core == 1, 12, NEAR + 1), slot_one, 0)
-    write_dq(y, 1)
+    lax.fori_loop(0, 12 * core, slot_one, 0)
     join(1)
 
     @pl.when(core == 0)
     def _():
         second_level()
 
+    write_dq(y, 1)
     join(0)
 
+    def fin(ref, slot, n):
+        return remote(ref.at[0, slot], ref.at[2, slot], s_fin.at[n, slot], r_fin.at[n, slot], sibling)
+
+    for part_half in range(2):
+        half = core if part_half == 1 else other
+        for g in range(GROUP):
+            fq[part_half, 1, g] = dq_part[y, 1, half, g]
+    fin(fq, 1, 0).start()
     for dy in range(1, COLUMNS):
         col = (y + dy) % 4
         remote(dq_part.at[0, 0], dq_in.at[col], s_dq.at[0], r_dq.at[col], sibling).wait_recv()
@@ -700,9 +730,7 @@
             for dy in range(1, COLUMNS):
                 total += dq_in[(y + dy) % 4, half, g].astype(F32)
             fq[part_half, 0, g] = total.astype(BF16)
-            fq[part_half, 1, g] = dq_part[y, 1, half, g]
-    q_fin = remote(fq.at[0], fq.at[2], s_fin.at[0], r_fin.at[0], sibling)
-    q_fin.start()
+    fin(fq, 0, 0).start()
 
     def add_near(block):
         near_back_landed(block).wait_recv()
@@ -742,15 +770,14 @@
                 rows = pl.ds(pl.multiple_of(half * ROWS, ROWS), ROWS)
                 acc, entry = (dkv_acc, 0) if slot == 0 else (dkv1_acc, home)
                 fkv[part_half, slot, part] = acc[part, entry, rows].astype(BF16)
-    kv_fin = remote(fkv.at[0], fkv.at[2], s_fin.at[1], r_fin.at[1], sibling)
-    kv_fin.start()
-    q_fin.wait_recv()
-    kv_fin.wait_recv()
+        fin(fkv, slot, 1).start()
+    for slot in range(2):
+        fin(fq, slot, 0).wait_recv()
 
     def entry(kind):
         return 1 + (core + kind // 2) % 2
 
-    for head in range(KV_HEADS):
+    def place_head(head, what):
         masks = [jnp.full((ROWS, HEAD_DIM), chosen_of[kind][head], jnp.int32) > 0 for kind in range(4)]
 
         def picked(read):
@@ -759,15 +786,27 @@
                 total = jnp.where(masks[kind], read(entry(kind), kind % 2).astype(F32), total)
             return total.astype(BF16)
 
-        for g in range(GROUP):
-            cols = slice((head * GROUP + g) * HEAD_DIM, (head * GROUP + g + 1) * HEAD_DIM)
-            dq_out[:, cols] = picked(lambda e, slot, g=g: fq[e, slot, g])
-        cols = slice(head * HEAD_DIM, (head + 1) * HEAD_DIM)
-        dk_out[:, cols] = picked(lambda e, slot: fkv[e, slot, 0])
-        dv_out[:, cols] = picked(lambda e, slot: fkv[e, slot, 1])
-
-    for c in sib_copies + [q_fin, kv_fin]:
+        if what == 0:
+            for g in range(GROUP):
+                cols = slice((head * GROUP + g) * HEAD_DIM, (head * GROUP + g + 1) * HEAD_DIM)
+                dq_out[:, cols] = picked(lambda e, slot, g=g: fq[e, slot, g])
+        else:
+            cols = slice(head * HEAD_DIM, (head + 1) * HEAD_DIM)
+            dk_out[:, cols] = picked(lambda e, slot: fkv[e, slot, 0])
+            dv_out[:, cols] = picked(lambda e, slot: fkv[e, slot, 1])
+
+    for head in range(KV_HEADS):
+        place_head(head, 0)
+    for slot in range(2):
+        fin(fkv, slot, 1).wait_recv()
+    for head in range(KV_HEADS):
+        place_head(head, 1)
+
+    for c in sib_copies:
         c.wait_send()
+    for slot in range(2):
+        fin(fq, slot, 0).wait_send()
+        fin(fkv, slot, 1).wait_send()
     for half in range(2):
         for c in q_forward(0, half):
             c.wait_send()
@@ -887,8 +926,8 @@
                 dma((PLANES,)),
                 dma((near_count,)),
                 dma((near_count,)),
-                dma((2,)),
-                dma((2,)),
+                dma((2, 2)),
+                dma((2, 2)),
             ],
             compiler_params=pltpu.CompilerParams(
                 collective_id=0, has_side_effects=True, vmem_limit_bytes=56 * 2**20

time: 72.1 us -> 70 us (0.971); the launches traced: 71.9 us -> 68.6 us
  Pallas kernels: 67.7 us -> 64.4 us
    pallas_call x1, Pallas kernels: 67.7 us -> 64.4 us  [per_device(): pl.pallas_call(kernel, in_specs=[pl.BlockSpec(memory_space=pltpu.SMEM)] +...]
where the time goes in v4:
time: 70 us; the launch traced here: 68.6 us
  Pallas kernels  64.4 us (92%)
  local copies, waits for them, and re-layouts  3.53 us (5%)
    pallas_call x1, Pallas kernels, per_device(): pl.pallas_call(kernel, in_specs=[pl.BlockSpec(memory_space=pltpu.SMEM)] +...  64.4 us
    unnamed x7, local copies, waits for them, and re-layouts  3.53 us

profile of v4, /device:TPU:103, one launch (start us, length us, event | category | flops | bytes accessed | tf_op | source)
XLA Modules:
  0.0 68.6 jit_solution(10886398393184318577)
XLA Ops:
  0.6 64.4 %gradients.1 = (bf16[128,2048]{1,0:T(8,128)(2,1)}, bf16[128,512]{1,0:T(8,128)(2,1)}, bf16[128,512]{1,0:T(8,128)(2,1)}) custom-call(s32[4]{0:T(128)} %spans_ref.1, bf16[128,2048]{1,0:T(8,128)(2,1)} %q_ref.1, bf16[128,512]{1,0:T(8,128)(2,1)} %k_ref.1, bf16[128,512]{1,0:T(8,128)(2,1)} %v_ref.1, bf16[128,2048]{1,0:T(8,128)(2,1)} %o_ref.1, ...), custom_call_target="tpu_custom_call" | custom-call | tf_op jit(solution)/shard_map/gradients/pallas_call | solution.py:882
  65.1 0.0 copy-start.1
  65.1 1.9 %copy.13 = bf16[128,2048]{1,0:T(8,128)(2,1)} copy(bf16[128,2048]{1,0:T(8,128)(2,1)} %get-tuple-element.6) | data formatting | bytes 1048576
  67.0 0.0 copy-done.1
  67.0 0.0 copy-start
  67.0 0.7 copy.14
  67.7 0.3 copy-done
  68.0 0.7 copy.15
Async XLA Ops:
  65.1 1.9 %copy-start.1 = (bf16[128,512]{1,0:T(8,128)(2,1)S(1)}, bf16[128,512]{1,0:T(8,128)(2,1)}, u32[]{:S(2)}) copy-start(bf16[128,512]{1,0:T(8,128)(2,1)} %get-tuple-element.7) | copy-start | bytes 393220
  67.0 1.0 %copy-start = (bf16[128,512]{1,0:T(8,128)(2,1)S(1)}, bf16[128,512]{1,0:T(8,128)(2,1)}, u32[]{:S(2)}) copy-start(bf16[128,512]{1,0:T(8,128)(2,1)} %get-tuple-element.8) | copy-start | bytes 393220

commit v5 on v4

--- a/solution.py
+++ b/solution.py
@@ -378,8 +378,11 @@
                 key = lax.broadcasted_iota(jnp.int32, (size, width), 0)
                 lane = lax.broadcasted_iota(jnp.int32, (size, width), 1)
                 row = lane % ROWS + lane // 512 * ROWS
-                distance = row - key + base
-                prob = jnp.where((distance >= 0) & (distance < own_limits[slot]), prob, 0.0)
+                ahead = row - key
+                seen_by = ahead < own_limits[slot] - base
+                if masked != "window":
+                    seen_by = seen_by & (ahead >= -base)
+                prob = jnp.where(seen_by, prob, 0.0)
             ds = (prob * (dot(v, g, NT) - stats(2))).astype(BF16)
             low = prob.astype(BF16)
             acc[0, into] += dot(ds, q).reshape(count, 256, HEAD_DIM)
@@ -586,7 +589,7 @@
 
         @pl.when(here & (i > full))
         def _():
-            tile(0, y, i, 1, True)
+            tile(0, y, i, 1, "window")
 
         @pl.when((core == 0) & (z >= 8 - i))
         def _():
@@ -660,7 +663,7 @@
         lax.fori_loop(0, below_count + above_count, plain, 0)
 
         def masked(d, cc):
-            tile(0, col, d, 1, True)
+            tile(0, col, d, 1, "window")
             return cc
 
         lax.fori_loop(jnp.maximum(full + 1, first), end + 1, masked, 0)

time: 70 us -> 69.3 us (0.990); the launches traced: 68.6 us -> 68.6 us
  no operation moved by 1% of the time
where the time goes in v5:
time: 69.3 us; the launch traced here: 68.6 us
  Pallas kernels  64.4 us (93%)
  local copies, waits for them, and re-layouts  3.53 us (5%)
    pallas_call x1, Pallas kernels, per_device(): pl.pallas_call(kernel, in_specs=[pl.BlockSpec(memory_space=pltpu.SMEM)] +...  64.4 us
    unnamed x7, local copies, waits for them, and re-layouts  3.53 us

profile of v5, /device:TPU:103, one launch (start us, length us, event | category | flops | bytes accessed | tf_op | source)
XLA Modules:
  0.0 68.6 jit_solution(18332222820360509720)
XLA Ops:
  0.6 64.4 %gradients.1 = (bf16[128,2048]{1,0:T(8,128)(2,1)}, bf16[128,512]{1,0:T(8,128)(2,1)}, bf16[128,512]{1,0:T(8,128)(2,1)}) custom-call(s32[4]{0:T(128)} %spans_ref.1, bf16[128,2048]{1,0:T(8,128)(2,1)} %q_ref.1, bf16[128,512]{1,0:T(8,128)(2,1)} %k_ref.1, bf16[128,512]{1,0:T(8,128)(2,1)} %v_ref.1, bf16[128,2048]{1,0:T(8,128)(2,1)} %o_ref.1, ...), custom_call_target="tpu_custom_call" | custom-call | tf_op jit(solution)/shard_map/gradients/pallas_call | solution.py:885
  65.1 0.0 copy-start.1
  65.1 1.9 %copy.13 = bf16[128,2048]{1,0:T(8,128)(2,1)} copy(bf16[128,2048]{1,0:T(8,128)(2,1)} %get-tuple-element.6) | data formatting | bytes 1048576
  67.0 0.0 copy-done.1
  67.0 0.0 copy-start
  67.0 0.7 copy.14
  67.7 0.3 copy-done
  68.0 0.7 copy.15
Async XLA Ops:
  65.1 1.9 %copy-start.1 = (bf16[128,512]{1,0:T(8,128)(2,1)S(1)}, bf16[128,512]{1,0:T(8,128)(2,1)}, u32[]{:S(2)}) copy-start(bf16[128,512]{1,0:T(8,128)(2,1)} %get-tuple-element.7) | copy-start | bytes 393220
  67.0 1.0 %copy-start = (bf16[128,512]{1,0:T(8,128)(2,1)S(1)}, bf16[128,512]{1,0:T(8,128)(2,1)}, u32[]{:S(2)}) copy-start(bf16[128,512]{1,0:T(8,128)(2,1)} %get-tuple-element.8) | copy-start | bytes 393220
